TPU v7x, 128 devices: a whole 4x4x4 slice. The times are simulated.
128 devices in a mesh: front: 8 (over x, core), row: 16 (over z, y).
Axes of the slice: x: 4, y: 4, z: 4, core: 2. Of those that a mesh axis runs over, the one named last changes fastest.
Arguments:
- parent: bfloat16 [8192, 8192], P(('front', 'row')), as said below
- margin: int32 [16, 16], P('front'), may hold values from 0 to 63, as said below
- counts: int32 [16], P('front'), may hold values from 8 to 16, as said below
- factor: bfloat16 [16, 2048, 4096], P('front', None, 'row'), may hold values from -0.125 to 0.125
- local_inverse: bfloat16 [16, 4096, 4096], P('front', None, 'row'), may hold values from -0.09375 to 0.09375
Outputs:
- coupling: bfloat16 [16, 2048, 4096], P('front', None, 'row')
- diag_blocks: float32 [16, 32, 128, 128], P('front', 'row')
Inputs may be any that keep to these rules, and one draw needn't show every extreme that they name: parent is exactly symmetric. The 16 entries of each row of margin are distinct. `counts`: some front has all 16 update blocks live.
All inputs are finite; a program needn't handle non-finite values.
Results may differ from a plain program's by a relative error of at most 0.0025.
Values may be sent and summed in bfloat16 or wider, within the bound.
A program may use at most 128 MiB of HBM per device.

v0:
```python
import jax
import jax.numpy as jnp
from jax import lax
from jax.sharding import PartitionSpec as P


def body(parent, margin, counts, factor, local_inverse):
    fronts_here, update, width_dev = factor.shape
    slot_count = margin.shape[1]
    block_size = update // slot_count
    front_order = local_inverse.shape[1]
    row_count = lax.axis_size("row")
    row_place = lax.axis_index("row")
    shard_rows = parent.shape[0]
    layers = lax.all_gather(parent, "front", axis=0, tiled=True)
    offsets = jnp.arange(block_size, dtype=jnp.int32)
    masked_pieces = []
    for front_index in range(fronts_here):
        global_ids = (margin[front_index][:, None] * block_size + offsets[None, :]).reshape(update)
        picked = jnp.take(layers, global_ids, axis=1)
        shard_ids = global_ids // shard_rows
        holder = shard_ids % row_count
        local_ids = shard_ids // row_count * shard_rows + global_ids % shard_rows
        selected = jnp.take(picked, local_ids, axis=0)
        owned_rows = holder == row_place
        masked_pieces.append(jnp.where(owned_rows[:, None], selected, jnp.zeros_like(selected)))
    sigmas = [
        lax.psum(masked_piece, "row").astype(jnp.float32).astype(jnp.bfloat16)
        for masked_piece in masked_pieces
    ]
    col_global = row_place * width_dev + jnp.arange(width_dev, dtype=jnp.int32)
    lower_mask = jnp.arange(front_order, dtype=jnp.int32)[:, None] >= col_global[None, :]
    block_of_row = jnp.arange(update, dtype=jnp.int32) // block_size
    col_blocks = width_dev // block_size
    couplings = []
    diagonals = []
    for front_index in range(fronts_here):
        live_rows = block_of_row < counts[front_index]
        front_factor = factor[front_index]
        live_factor = jnp.where(live_rows[:, None], front_factor, jnp.zeros_like(front_factor))
        product = jnp.dot(sigmas[front_index], live_factor, preferred_element_type=jnp.float32)
        coupling = jnp.where(live_rows[:, None], -product, jnp.zeros_like(product)).astype(
            jnp.bfloat16
        )
        front_inverse = local_inverse[front_index]
        triangle = jnp.where(lower_mask, front_inverse, jnp.zeros_like(front_inverse)).reshape(
            front_order, col_blocks, block_size
        )
        local_term = jnp.einsum(
            "kcx,kcy->cxy", triangle, triangle, preferred_element_type=jnp.float32
        )
        factor_blocks = live_factor.reshape(update, col_blocks, block_size)
        coupling_blocks = coupling.reshape(update, col_blocks, block_size)
        cross_term = jnp.einsum(
            "rcx,rcy->cxy", factor_blocks, coupling_blocks, preferred_element_type=jnp.float32
        )
        couplings.append(coupling)
        diagonals.append(local_term - cross_term)
    return (jnp.stack(couplings), jnp.stack(diagonals))


def solution(mesh):
    placed = (
        P(("front", "row"), None),
        P("front", None),
        P("front"),
        P("front", None, "row"),
        P("front", None, "row"),
    )
    return jax.shard_map(
        body,
        mesh=mesh,
        in_specs=placed,
        out_specs=(P("front", None, "row"), P("front", "row", None, None)),
        check_vma=False,
    )
```

profile of v0, /device:TPU:0, one launch (start us, length us, event | category | flops | bytes accessed | tf_op | source)
XLA Modules:
  0.0 396.8 jit_solution(13861941372243377463)
XLA Ops:
  7.2 0.0 all-gather.2.cloned.1.call-start
  7.2 0.7 all-gather.2.cloned.1.call-update
  7.9 0.0 all-reduce.3.cloned.1.call-start
  7.9 0.8 multiply_bitcast_fusion.1
  8.7 0.1 fusion.26
  8.9 0.1 fusion.38
  8.9 53.0 %all-gather.2.cloned.1.call-done = bf16[512,8192]{1,0:T(8,128)(2,1)} async-done(((bf16[64,8192]{1,0:T(8,128)(2,1)}), bf16[512,8192]{1,0:T(8,128)(2,1)}) %all-gather.2.cloned.1.call-update) | async-done | bytes 8388624 | tf_op jit(solution)/shard_map/all_gather | solution.py:15
  61.9 11.4 %copy.19 = bf16[512,8192]{0,1:T(8,128)(2,1)} copy(bf16[512,8192]{1,0:T(8,128)(2,1)} %all-gather.2.cloned.1.call-done) | data formatting | bytes 16777216 | tf_op jit(solution)/shard_map/all_gather | solution.py:15
  73.3 12.0 %gather_fusion = bf16[2048,512]{1,0:T(8,128)(2,1)S(1)} fusion(bf16[512,8192]{0,1:T(8,128)(2,1)} %copy.19, s32[2048]{0:T(1024)S(1)} %get-tuple-element.35), kind=kCustom, calls=%fused_computation.clone | custom fusion | bytes 4202496 | tf_op jit(solution)/shard_map/jit(_take)/gather | solution.py:20
  85.4 1.5 select_bitcast_fusion.1
  86.9 2.9 copy.20
  89.9 13.7 %gather_fusion.2 = bf16[2048,512]{1,0:T(8,128)(2,1)} fusion(bf16[512,8192]{0,1:T(8,128)(2,1)} %copy.19, s32[2048]{0:T(1024)S(1)} %get-tuple-element.34), kind=kCustom, calls=%fused_computation.2.clone | custom fusion | bytes 4202496 | tf_op jit(solution)/shard_map/jit(_take)/gather | solution.py:20
  103.6 2.7 select_bitcast_fusion
  106.3 4.0 %copy.23 = bf16[512,2048]{1,0:T(8,128)(2,1)} copy(bf16[512,2048]{0,1:T(8,128)(2,1)} %select_bitcast_fusion) | data formatting | bytes 4194304 | tf_op jit(solution)/shard_map/jit(_take)/select_n | solution.py:20
  110.3 11.1 %gather_fusion.1 = bf16[2048,2048]{1,0:T(8,128)(2,1)} fusion(bf16[512,2048]{1,0:T(8,128)(2,1)S(1)} %copy.20, s32[2048]{0:T(1024)S(1)} %broadcast_clamp_fusion.1), kind=kCustom, calls=%fused_computation.1.clone | custom fusion | bytes 16785408 | tf_op jit(solution)/shard_map/jit(_take)/gather | solution.py:24
  121.4 18.2 %gather_fusion.3 = bf16[2048,2048]{1,0:T(8,128)(2,1)} fusion(bf16[512,2048]{1,0:T(8,128)(2,1)} %copy.23, s32[2048]{0:T(1024)S(1)} %broadcast_clamp_fusion), kind=kCustom, calls=%fused_computation.3.clone | custom fusion | bytes 16785408 | tf_op jit(solution)/shard_map/jit(_take)/gather | solution.py:24
  139.6 0.0 slice-start
  139.6 0.0 slice-start.1
  139.6 9.0 %select_select_fusion.1 = bf16[2048,2048]{1,0:T(8,128)(2,1)} fusion(bf16[2048,2048]{1,0:T(8,128)(2,1)} %gather_fusion.1, pred[2048]{0:T(1024)(128)(4,1)S(1)} %get-tuple-element.24, pred[2048]{0:T(1024)(128)(4,1)S(1)} %get-tuple-element.22), kind=kLoop, calls=%fused_computation.5 | loop fusion | flops 8388608 | bytes 16781312 | tf_op jit(solution)/shard_map/jit(_where)/select_n | solution.py:26
  148.6 0.0 slice-done
  148.6 0.0 slice-done.1
  148.6 4.5 %select_select_fusion = bf16[2048,2048]{1,0:T(8,128)(2,1)} fusion(bf16[2048,2048]{1,0:T(8,128)(2,1)S(1)} %bitcast.149, pred[2048]{0:T(1024)(128)(4,1)S(1)} %get-tuple-element.30, pred[2048]{0:T(1024)(128)(4,1)S(1)} %get-tuple-element.33), kind=kLoop, calls=%fused_computation.4 | loop fusion | flops 8388608 | bytes 16781312 | tf_op jit(solution)/shard_map/jit(_where)/select_n | solution.py:26
  153.1 0.0 all-reduce.3.cloned.1.call-update
  153.1 1.7 fusion.64
  154.8 1.4 copy.39
  156.2 3.8 fusion.63
  160.0 4.2 %copy.37 = bf16[1,4096,256]{1,2,0:T(8,128)(2,1)} copy(bf16[1,4096,256]{2,1,0:T(8,128)(2,1)} %get-tuple-element.15) | data formatting | bytes 4194304 | tf_op jit(solution)/shard_map/squeeze | solution.py:45
  164.2 1.4 copy.38
  165.6 0.0 copy-start.7
  165.6 2.8 copy.36
  168.5 0.0 copy-done.7
  168.5 0.6 fusion.65
  169.1 0.6 fusion.34
  169.7 0.7 fusion.35
  170.4 0.0 copy-start
  170.4 3.4 fusion.8
  173.8 0.0 copy-done
  173.8 0.0 copy-start.1
  173.8 0.9 fusion.6
  174.7 200.1 %all-reduce.3.cloned.1.call-done = (bf16[2048,2048]{1,0:T(8,128)(2,1)}, bf16[2048,2048]{1,0:T(8,128)(2,1)}) async-done(((bf16[2048,2048]{1,0:T(8,128)(2,1)}, bf16[2048,2048]{1,0:T(8,128)(2,1)}), (bf16[2048,2048]{1,0:T(8,128)(2,1)}, bf16[2048,2048]{1,0:T(8,128)(2,1)})) %all-reduce.3.cloned.1.call-update) | async-done | bytes 16777232 | tf_op jit(solution)/shard_map/psum | solution.py:28
  374.8 0.0 copy-done.1
  374.8 0.0 copy-start.2
  374.8 0.0 copy-start.8
  374.8 5.9 %fusion.4 = bf16[2048,256]{0,1:T(8,128)(2,1)S(1)} fusion(bf16[2048,2048]{1,0:T(8,128)(2,1)} %get-tuple-element.8, bf16[1,2048,256]{1,2,0:T(8,128)(2,1)S(1)} %copy-done.1, pred[2048]{0:T(1024)(128)(4,1)S(1)} %fusion.34), kind=kOutput, calls=%fused_computation.13 | convolution fusion | flops 2149580800 | bytes 10487808 | tf_op jit(solution)/shard_map/dot_general | solution.py:41
  380.7 0.0 copy-start.6
  380.7 0.0 copy-done.2
  380.7 0.2 copy-done.8
  380.9 2.4 fusion.5
  383.3 0.0 copy-start.4
  383.3 0.0 copy-done.6
  383.3 1.0 copy-done.4
  384.3 0.2 pad_maximum_fusion
  384.5 2.5 copy.31
  387.0 0.0 copy-start.3
  387.0 0.0 copy-start.5
  387.0 1.8 fusion.12
  388.8 0.0 copy-done.3
  388.8 0.0 copy-done.5
  388.8 0.4 fusion.13
  389.3 0.7 pad_maximum_fusion.1
  (4 shorter events, 0.0 us)
Async XLA Ops:
  7.2 54.7 %all-gather.2.cloned.1.call-start = ((), (), s32[]{:S(2)}) async-start(), calls=%async_computation | async-start | bytes 9437184 | tf_op jit(solution)/shard_map/all_gather | solution.py:15
  7.9 366.9 %all-reduce.3.cloned.1.call-start = ((), (), s32[]{:S(2)}) async-start(), calls=%async_computation.1 | async-start | bytes 33554432 | tf_op jit(solution)/shard_map/psum | solution.py:28
  139.6 9.0 %slice-start = ((s8[8388608]{0:T(1024)(128)(4,1)}), s8[4194304]{0:T(1024)(128)(4,1)S(1)}, s32[]{:S(2)}) async-start(s8[8388608]{0:T(1024)(128)(4,1)} %bitcast.148), calls=%async_computation.2 | async-start | bytes 8388608
  139.6 9.0 %slice-start.1 = ((s8[8388608]{0:T(1024)(128)(4,1)}), s8[4194304]{0:T(1024)(128)(4,1)S(1)}, s32[]{:S(2)}) async-start(s8[8388608]{0:T(1024)(128)(4,1)} %bitcast.148), calls=%async_computation.3 | async-start | bytes 8388608
  165.6 2.9 copy-start.7
  170.4 3.4 copy-start
  173.8 201.0 %copy-start.1 = (bf16[1,2048,256]{1,2,0:T(8,128)(2,1)S(1)}, bf16[1,2048,256]{1,2,0:T(8,128)(2,1)}, u32[]{:S(2)}) copy-start(bf16[1,2048,256]{1,2,0:T(8,128)(2,1)} %copy.39) | copy-start | bytes 3145732
  374.8 5.9 %copy-start.2 = (bf16[1,2048,256]{1,2,0:T(8,128)(2,1)S(1)}, bf16[1,2048,256]{1,2,0:T(8,128)(2,1)}, u32[]{:S(2)}) copy-start(bf16[1,2048,256]{1,2,0:T(8,128)(2,1)} %copy.38) | copy-start | bytes 3145732
  374.8 6.1 %copy-start.8 = (bf16[2048,2048]{1,0:T(8,128)(2,1)S(1)}, bf16[2048,2048]{1,0:T(8,128)(2,1)}, u32[]{:S(2)}) copy-start(bf16[2048,2048]{1,0:T(8,128)(2,1)} %get-tuple-element.9) | copy-start | bytes 25165828
  380.7 2.6 copy-start.6
  383.3 1.0 copy-start.4
  387.0 1.8 copy-start.3
  387.0 1.9 copy-start.5
Sparse Core Ops, SparseCore 0:
  9.7 52.1 all-gather.1
  153.2 221.5 all-reduce.2
where the time goes:
time: 398 us; the launch traced here: 397 us
  waiting for transfers between devices  254 us (64%)
  local copies, waits for them, and re-layouts  93.1 us (23%)
  other arithmetic  20.9 us (5%)
  matrix products  14.8 us (4%)
  between operations  14.2 us (4%)
    psum x1, waiting for transfers between devices, body(): lax.psum(masked_piece, 'row').astype(jnp.float32).astype(jnp.bfloat16)  200 us
    all_gather x1, waiting for transfers between devices, body(): layers = lax.all_gather(parent, 'front', axis=0, tiled=True)  53 us
    gather x2, local copies, waits for them, and re-layouts, body(): selected = jnp.take(picked, local_ids, axis=0)  29.3 us
    gather x2, local copies, waits for them, and re-layouts, body(): picked = jnp.take(layers, global_ids, axis=1)  25.8 us
    select_n x2, other arithmetic, body(): jnp.where(owned_rows[:, None], selected, jnp.zeros_like(selected))  13.4 us
    all_gather x1, local copies, waits for them, and re-layouts, body(): layers = lax.all_gather(parent, 'front', axis=0, tiled=True)  11.4 us
    dot_general x2, matrix products, body(): jnp.dot(sigmas[front_index], live_factor, preferred_element_type=jnp.floa...  8.27 us
  transfers between devices with their start and end apart: 2, of which 2 were waited for; matrix products, arithmetic and copies ran while one was open for 6% of the time, Pallas kernels for 0%

commit v1 on v0

v1 whole, which is shorter than its diff:
```python
import functools

import jax
import jax.numpy as jnp
from jax import lax
from jax.experimental import pallas as pl
from jax.experimental.pallas import tpu as pltpu
from jax.sharding import PartitionSpec as P

MESH = pl.DeviceIdType.MESH
NOV = 16
BLOCK = 128
BAND = 9
SLICES = 64


def place(x, core, y, z):
    return (2 * x + core, 4 * z + y)


def gather_kernel(
    parent_ref, margin_ref, out_ref,
    slabs, picked, margin_buf, margin_smem,
    t_send, t_recv, d_send, d_recv, m_send, m_recv, l_sem, x_send, x_recv, g_send, g_recv,
):
    front = lax.axis_index("front")
    row = lax.axis_index("row")
    x, core = front // 2, front % 2
    z, y = row // 4, row % 4
    half, yh = y % 2, y // 2
    me_q = yh * 16 + z * 4 + x
    my_block = 16 * x + 8 * core + 2 * z + yh
    my_slice = half * 32 + me_q
    sibling = place(x, 1 - core, y, z)
    y_up = place(x, core, (y + 1) % 4, z)
    y_down = place(x, core, (y + 3) % 4, z)
    z_up = place(x, core, y, (z + 1) % 4)
    z_down = place(x, core, y, (z + 3) % 4)

    def member(q):
        return place(q % 4, core, 2 * (q // 16) + half, (q // 4) % 4)

    barrier = pltpu.get_barrier_semaphore()

    def greet(step, _):
        pl.semaphore_signal(
            barrier, inc=1, device_id=member((me_q + step) % 32), device_id_type=MESH
        )
        return 0

    lax.fori_loop(1, 32, greet, 0)
    for other in (sibling, y_up, y_down):
        pl.semaphore_signal(barrier, inc=1, device_id=other, device_id_type=MESH)
    pl.semaphore_wait(barrier, 34)

    margin_sends = []
    for step in (1, 2, 3):
        copy = pltpu.make_async_remote_copy(
            src_ref=margin_ref,
            dst_ref=margin_buf.at[x],
            send_sem=m_send.at[step],
            recv_sem=m_recv.at[x],
            device_id=place((x + step) % 4, core, y, z),
            device_id_type=MESH,
        )
        copy.start()
        margin_sends.append(copy)
    own_margin = pltpu.make_async_copy(margin_ref, margin_buf.at[x], m_recv.at[x])
    own_margin.start()

    own_slab = pltpu.make_async_copy(
        parent_ref.at[me_q // 4, :, me_q % 4], slabs.at[my_block], t_recv.at[x]
    )
    own_slab.start()

    def spread(step, _):
        q = (me_q + step) % 32
        pltpu.make_async_remote_copy(
            src_ref=parent_ref.at[q // 4, :, q % 4],
            dst_ref=slabs.at[my_block],
            send_sem=t_send,
            recv_sem=t_recv.at[x],
            device_id=member(q),
            device_id_type=MESH,
        ).start()
        return 0

    lax.fori_loop(1, 32, spread, 0)

    for source in range(4):
        pltpu.make_async_copy(margin_ref, margin_buf.at[source], m_recv.at[source]).wait()
    to_smem = pltpu.make_async_copy(margin_buf, margin_smem, l_sem.at[0])
    to_smem.start()

    exchanges = []
    for source in range(4):
        group = slabs.at[pl.ds(16 * source + 8 * core, 8)]
        pltpu.make_async_copy(group, group, t_recv.at[source]).wait()
        copy = pltpu.make_async_remote_copy(
            src_ref=group,
            dst_ref=group,
            send_sem=d_send.at[source],
            recv_sem=d_recv.at[source],
            device_id=sibling,
            device_id_type=MESH,
        )
        copy.start()
        exchanges.append(copy)
    to_smem.wait()
    for copy in exchanges:
        copy.wait()

    x_copies = []
    for step in (2, 1, 3, 0):
        target = (x + step) % 4

        def pick(index, _):
            part, a = index // NOV, index % NOV
            block_row = margin_smem[target, part, a]
            for d in range(BAND):
                block_col = margin_smem[target, part, a + d]
                picked[target, part, a, d] = slabs[block_row, block_col]
            return 0

        lax.fori_loop(0, 2 * NOV, pick, 0)
        if step:
            copy = pltpu.make_async_remote_copy(
                src_ref=picked.at[target],
                dst_ref=out_ref.at[:, :, :, my_slice],
                send_sem=x_send.at[step],
                recv_sem=x_recv.at[4 - step],
                device_id=place(target, core, y, z),
                device_id_type=MESH,
            )
        else:
            copy = pltpu.make_async_copy(
                picked.at[target], out_ref.at[:, :, :, my_slice], l_sem.at[1]
            )
        copy.start()
        x_copies.append(copy)
    for copy in x_copies:
        copy.wait()

    def y_chunk(part, lo, size, y_at):
        first = (y_at % 2) * 32 + (y_at // 2) * 16 + z * 4
        return out_ref.at[part, pl.ds(lo, size), :, pl.ds(first, 4)]

    def z_slab(part, lo, size, z_at):
        return [
            out_ref.at[part, pl.ds(lo, size), :, pl.ds(o * 16 + z_at * 4, 4)] for o in range(4)
        ]

    def z_chunk(part, lo, size, z_at):
        first = half * 32 + yh * 16 + z_at * 4
        return out_ref.at[part, pl.ds(lo, size), :, pl.ds(first, 4)]

    def y_slab(part, lo, size, y_at):
        first = (y_at % 2) * 32 + (y_at // 2) * 16
        return out_ref.at[part, pl.ds(lo, size), :, pl.ds(first, 16)]

    def send(ref, slot, device):
        copy = pltpu.make_async_remote_copy(
            src_ref=ref, dst_ref=ref, send_sem=g_send.at[slot], recv_sem=g_recv.at[slot],
            device_id=device, device_id_type=MESH,
        )
        copy.start()
        return copy

    def landed(ref, slot):
        pltpu.make_async_copy(ref, ref, g_recv.at[slot]).wait()

    up_y, down_y = (y + 1) % 4, (y + 3) % 4
    up_z, down_z = (z + 1) % 4, (z + 3) % 4
    sends = []
    sends.append(send(y_chunk(0, 0, NOV, y), 0, y_up))
    sends.append(send(z_chunk(1, 0, NOV, z), 1, z_up))
    sends.append(send(y_chunk(0, 0, NOV, y), 2, y_down))
    sends.append(send(z_chunk(1, 0, NOV, z), 3, z_down))
    landed(y_chunk(0, 0, NOV, down_y), 0)
    sends.append(send(y_chunk(0, 0, 8, down_y), 4, y_up))
    landed(z_chunk(1, 0, NOV, down_z), 1)
    sends.append(send(z_chunk(1, 0, 8, down_z), 5, z_up))
    landed(y_chunk(0, 0, NOV, up_y), 2)
    sends.append(send(y_chunk(0, 8, 8, up_y), 6, y_down))
    landed(z_chunk(1, 0, NOV, up_z), 3)
    sends.append(send(z_chunk(1, 8, 8, up_z), 7, z_down))
    far_y, far_z = (y + 2) % 4, (z + 2) % 4
    landed(y_chunk(0, 0, 8, far_y), 4)
    landed(y_chunk(0, 8, 8, far_y), 6)
    landed(z_chunk(1, 0, 8, far_z), 5)
    landed(z_chunk(1, 8, 8, far_z), 7)

    def send_slab(pieces, slot, device):
        for o, piece in enumerate(pieces):
            sends.append(send(piece, slot + o, device))

    def slab_landed(pieces, slot):
        for o, piece in enumerate(pieces):
            landed(piece, slot + o)

    send_slab(z_slab(0, 0, NOV, z), 8, z_up)
    sends.append(send(y_slab(1, 0, NOV, y), 24, y_up))
    send_slab(z_slab(0, 0, NOV, z), 12, z_down)
    sends.append(send(y_slab(1, 0, NOV, y), 25, y_down))
    slab_landed(z_slab(0, 0, NOV, down_z), 8)
    send_slab(z_slab(0, 0, 8, down_z), 16, z_up)
    landed(y_slab(1, 0, NOV, down_y), 24)
    sends.append(send(y_slab(1, 0, 8, down_y), 26, y_up))
    slab_landed(z_slab(0, 0, NOV, up_z), 12)
    send_slab(z_slab(0, 8, 8, up_z), 20, z_down)
    landed(y_slab(1, 0, NOV, up_y), 25)
    sends.append(send(y_slab(1, 8, 8, up_y), 27, y_down))
    slab_landed(z_slab(0, 0, 8, far_z), 16)
    slab_landed(z_slab(0, 8, 8, far_z), 20)
    landed(y_slab(1, 0, 8, far_y), 26)
    landed(y_slab(1, 8, 8, far_y), 27)

    for copy in sends:
        copy.wait_send()
    for copy in margin_sends:
        copy.wait_send()
    sent = slabs.at[pl.ds(0, 31)]
    pltpu.make_async_copy(sent, sent, t_send).wait()


def gathered(parent, margin):
    grid = parent.reshape(8, 4, 2, 64, BLOCK).transpose(0, 3, 1, 2, 4)
    wide = jnp.concatenate([margin, margin], axis=1)
    wide = jnp.pad(wide, ((0, 6), (0, 128 - 2 * NOV)))
    dma = pltpu.SemaphoreType.DMA
    return pl.pallas_call(
        gather_kernel,
        out_shape=jax.ShapeDtypeStruct((2, NOV, BAND, SLICES, 2, BLOCK), jnp.bfloat16),
        in_specs=[pl.BlockSpec(memory_space=pl.ANY), pl.BlockSpec(memory_space=pltpu.VMEM)],
        out_specs=pl.BlockSpec(memory_space=pltpu.VMEM),
        scratch_shapes=[
            pltpu.VMEM((64, 64, 2, BLOCK), jnp.bfloat16),
            pltpu.VMEM((4, 2, NOV, BAND, 2, BLOCK), jnp.bfloat16),
            pltpu.VMEM((4, 8, 128), jnp.int32),
            pltpu.SMEM((4, 8, 128), jnp.int32),
            dma, dma((4,)), dma((4,)), dma((4,)), dma((4,)), dma((4,)), dma((2,)),
            dma((4,)), dma((4,)), dma((28,)), dma((28,)),
        ],
        compiler_params=pltpu.CompilerParams(
            collective_id=0, has_side_effects=True, vmem_limit_bytes=40 * 2**20
        ),
        cost_estimate=pl.CostEstimate(flops=0, bytes_accessed=10 * 2**20, transcendentals=0),
    )(grid, wide)


def update_kernel(counts_ref, sub_ref, factor_ref, inverse_ref, coupling_ref, diag_ref, live):
    count = counts_ref[pl.program_id(0)]
    first_col = lax.axis_index("row") * 256

    def mask(a, _):
        rows = pl.multiple_of(a * BLOCK, BLOCK)
        value = factor_ref[0, pl.ds(rows, BLOCK), :]
        value = jnp.where(a < count, value, jnp.zeros_like(value))
        live[pl.ds(rows, BLOCK), :] = value
        live[pl.ds(rows + NOV * BLOCK, BLOCK), :] = value
        return 0

    lax.fori_loop(0, NOV, mask, 0)

    def block_row(a, _):
        rows = pl.multiple_of(a * BLOCK, BLOCK)
        direct = jnp.concatenate([sub_ref[0, a, d] for d in range(BAND)], axis=1)
        total = jnp.dot(
            direct, live[pl.ds(rows, BAND * BLOCK), :], preferred_element_type=jnp.float32
        )
        mirrored = jnp.concatenate(
            [sub_ref[0, (a + NOV - d) % NOV, d] for d in range(7, 0, -1)], axis=0
        )
        total += lax.dot_general(
            mirrored, live[pl.ds(rows + 9 * BLOCK, 7 * BLOCK), :],
            (((0,), (0,)), ((), ())), preferred_element_type=jnp.float32,
        )
        total = jnp.where(a < count, -total, jnp.zeros_like(total))
        coupling_ref[0, pl.ds(rows, BLOCK), :] = total.astype(jnp.bfloat16)
        return 0

    lax.fori_loop(0, NOV, block_row, 0)

    def local(step, total):
        rows = pl.multiple_of(step * 512, 512)
        value = inverse_ref[0, pl.ds(rows, 512), :]
        row_at = rows + lax.broadcasted_iota(jnp.int32, value.shape, 0)
        col_at = first_col + lax.broadcasted_iota(jnp.int32, value.shape, 1)
        value = jnp.where(row_at >= col_at, value, jnp.zeros_like(value))
        return total + lax.dot_general(
            value, value, (((0,), (0,)), ((), ())), preferred_element_type=jnp.float32
        )

    total = lax.fori_loop(0, 8, local, jnp.zeros((256, 256), jnp.float32))

    def cross(step, total):
        rows = pl.multiple_of(step * 512, 512)
        return total - lax.dot_general(
            live[pl.ds(rows, 512), :], coupling_ref[0, pl.ds(rows, 512), :],
            (((0,), (0,)), ((), ())), preferred_element_type=jnp.float32,
        )

    total = lax.fori_loop(0, 4, cross, total)
    for c in range(2):
        at = slice(c * BLOCK, (c + 1) * BLOCK)
        diag_ref[0, c] = total[at, at]


def body(parent, margin, counts, factor, local_inverse):
    sub = gathered(parent, margin).reshape(2, NOV, BAND, BLOCK, BLOCK)
    return pl.pallas_call(
        update_kernel,
        grid=(2,),
        out_shape=(
            jax.ShapeDtypeStruct(factor.shape, jnp.bfloat16),
            jax.ShapeDtypeStruct((2, 2, BLOCK, BLOCK), jnp.float32),
        ),
        in_specs=[
            pl.BlockSpec(memory_space=pltpu.SMEM),
            pl.BlockSpec((1, NOV, BAND, BLOCK, BLOCK), lambda f: (f, 0, 0, 0, 0)),
            pl.BlockSpec((1, 2048, 256), lambda f: (f, 0, 0)),
            pl.BlockSpec((1, 4096, 256), lambda f: (f, 0, 0)),
        ],
        out_specs=(
            pl.BlockSpec((1, 2048, 256), lambda f: (f, 0, 0)),
            pl.BlockSpec((1, 2, BLOCK, BLOCK), lambda f: (f, 0, 0, 0)),
        ),
        scratch_shapes=[pltpu.VMEM((4096, 256), jnp.bfloat16)],
        compiler_params=pltpu.CompilerParams(vmem_limit_bytes=40 * 2**20),
        cost_estimate=pl.CostEstimate(
            flops=6 * 10**9, bytes_accessed=20 * 2**20, transcendentals=0
        ),
    )(counts, sub, factor, local_inverse)


def solution(mesh):
    placed = (
        P(("front", "row"), None),
        P("front", None),
        P("front"),
        P("front", None, "row"),
        P("front", None, "row"),
    )
    return jax.shard_map(
        body,
        mesh=mesh,
        in_specs=placed,
        out_specs=(P("front", None, "row"), P("front", "row", None, None)),
        check_vma=False,
    )
```

time: 398 us -> 122 us (0.31)
  waiting for transfers between devices: 254 us -> 0 us
  Pallas kernels: 0 us -> 116 us
  local copies, waits for them, and re-layouts: 93.1 us -> 4.85 us
  other arithmetic: 20.9 us -> 0.83 us
  matrix products: 14.8 us -> 0 us
  between operations: 14.2 us -> 0.65 us
    psum x1 -> x0, waiting for transfers between devices: 200 us -> none  [body(): lax.psum(masked_piece, 'row').astype(jnp.float32).astype(jnp.bfloat16)]
    pallas_call x0 -> x2, Pallas kernels: none -> 116 us  [the longest x1 93.6 us: gathered(): pl.pallas_call(gather_kernel, out_shape=jax.ShapeDtypeStruct((2, NOV, BAN...]
    gather x4 -> x0, local copies, waits for them, and re-layouts: 55.1 us -> none  [the longest x2 29.3 us: body(): selected = jnp.take(picked, local_ids, axis=0)]
    all_gather x1 -> x0, waiting for transfers between devices: 53 us -> none  [body(): layers = lax.all_gather(parent, 'front', axis=0, tiled=True)]
    select_n x4 -> x0, other arithmetic: 17.7 us -> none  [the longest x2 13.4 us: body(): jnp.where(owned_rows[:, None], selected, jnp.zeros_like(selected))]
    dot_general x6 -> x0, matrix products: 14.8 us -> none  [the longest x2 8.27 us: body(): jnp.dot(sigmas[front_index], live_factor, preferred_element_type=jnp.floa...]
    all_gather x1 -> x0, local copies, waits for them, and re-layouts: 11.4 us -> none  [body(): layers = lax.all_gather(parent, 'front', axis=0, tiled=True)]
    squeeze x2 -> x0, local copies, waits for them, and re-layouts: 7.03 us -> none  [body(): front_inverse = local_inverse[front_index]]
  transfers between devices with their start and end apart: 2 -> 0, of which waited for: 2 -> 0; matrix products, arithmetic and copies ran while one was open for 6% -> 0% of each run, Pallas kernels for 0% -> 0%
where the time goes in v1:
time: 122 us
  Pallas kernels  116 us (95%)
  local copies, waits for them, and re-layouts  4.85 us (4%)
    pallas_call x1, Pallas kernels, gathered(): pl.pallas_call(gather_kernel, out_shape=jax.ShapeDtypeStruct((2, NOV, BAN...  93.6 us
    pallas_call x1, Pallas kernels, body(): pl.pallas_call(update_kernel, grid=(2,), out_shape=(jax.ShapeDtypeStruct(...  22.4 us
    unnamed x10, local copies, waits for them, and re-layouts  4.85 us

profile of v1, /device:TPU:0, one launch (start us, length us, event | category | flops | bytes accessed | tf_op | source)
XLA Modules:
  0.0 122.3 jit_solution(15004534105914986564)
XLA Ops:
  0.6 0.8 pad_add_fusion
  1.5 0.0 copy-start.1
  1.5 1.2 %copy-done.1 = bf16[64,8192]{1,0:T(8,128)(2,1)S(1)} copy-done((bf16[64,8192]{1,0:T(8,128)(2,1)S(1)}, bf16[64,8192]{1,0:T(8,128)(2,1)}, u32[]{:S(2)}) %copy-start.1) | copy-done | bytes 1048600
  2.7 0.0 copy-start.2
  2.7 0.0 copy-start.3
  2.7 0.0 copy-start.4
  2.7 93.6 %shard_map.68 = bf16[2,16,9,64,2,128]{5,4,3,2,1,0:T(2,128)(2,1)S(1)} custom-call(bf16[8,64,4,2,128]{4,3,2,1,0:T(2,128)(2,1)S(1)} %bitcast.5, s32[8,128]{1,0:T(8,128)S(1)} %pad.4.margin_ref), custom_call_target="tpu_custom_call" | custom-call | bytes 10485760 | tf_op jit(solution)/shard_map/pallas_call | solution.py:231
  96.3 0.0 copy-start
  96.3 3.6 %copy-done = bf16[2,16,9,64,2,128]{5,4,3,2,1,0:T(2,128)(2,1)} copy-done((bf16[2,16,9,64,2,128]{5,4,3,2,1,0:T(2,128)(2,1)}, bf16[2,16,9,64,2,128]{5,4,3,2,1,0:T(2,128)(2,1)S(1)}, u32[]{:S(2)}) %copy-start) | copy-done | bytes 9437208
  99.9 0.0 copy-done.2
  99.9 0.0 copy-done.3
  99.9 0.0 copy-done.4
  99.9 22.4 %shard_map.69 = (bf16[2,2048,256]{2,1,0:T(8,128)(2,1)}, f32[2,2,128,128]{3,2,1,0:T(8,128)}) custom-call(s32[2]{0:T(128)S(1)} %copy-done.4, bf16[2,16,9,128,128]{4,3,2,1,0:T(8,128)(2,1)} %bitcast.4, bf16[2,2048,256]{2,1,0:T(8,128)(2,1)S(1)} %copy-done.3, bf16[2,4096,256]{2,1,0:T(8,128)(2,1)S(1)} %copy-done.2), custom_call_target="tpu_custom_call" | custom-call | flops 6000000000 | bytes 20971520 | tf_op jit(solution)/shard_map/pallas_call | solution.py:311
  (1 shorter events, 0.0 us)
Async XLA Ops:
  1.5 1.2 %copy-start.1 = (bf16[64,8192]{1,0:T(8,128)(2,1)S(1)}, bf16[64,8192]{1,0:T(8,128)(2,1)}, u32[]{:S(2)}) copy-start(bf16[64,8192]{1,0:T(8,128)(2,1)} %param.5) | copy-start | bytes 3145732
  2.7 97.2 %copy-start.2 = (bf16[2,4096,256]{2,1,0:T(8,128)(2,1)S(1)}, bf16[2,4096,256]{2,1,0:T(8,128)(2,1)}, u32[]{:S(2)}) copy-start(bf16[2,4096,256]{2,1,0:T(8,128)(2,1)} %inverse_ref.1) | copy-start | bytes 12582916
  2.7 97.2 %copy-start.3 = (bf16[2,2048,256]{2,1,0:T(8,128)(2,1)S(1)}, bf16[2,2048,256]{2,1,0:T(8,128)(2,1)}, u32[]{:S(2)}) copy-start(bf16[2,2048,256]{2,1,0:T(8,128)(2,1)} %factor_ref.1) | copy-start | bytes 6291460
  2.7 97.2 %copy-start.4 = (s32[2]{0:T(128)S(1)}, s32[2]{0:T(128)}, u32[]{:S(2)}) copy-start(s32[2]{0:T(128)} %counts_ref.1) | copy-start | bytes 28
  96.3 3.6 %copy-start = (bf16[2,16,9,64,2,128]{5,4,3,2,1,0:T(2,128)(2,1)}, bf16[2,16,9,64,2,128]{5,4,3,2,1,0:T(2,128)(2,1)S(1)}, u32[]{:S(2)}) copy-start(bf16[2,16,9,64,2,128]{5,4,3,2,1,0:T(2,128)(2,1)S(1)} %shard_map.68) | copy-start | bytes 28311556

commit v2 on v1

v2 whole, which is shorter than its diff:
```python
import functools

import jax
import jax.numpy as jnp
from jax import lax
from jax.experimental import pallas as pl
from jax.experimental.pallas import tpu as pltpu
from jax.sharding import PartitionSpec as P

MESH = pl.DeviceIdType.MESH
NOV = 16
BLOCK = 128
CHUNKS = 4
ROWS = NOV // CHUNKS


def place(x, core, y, z):
    return (2 * x + core, 4 * z + y)


def band(chunk):
    return 9 if chunk < CHUNKS // 2 else 8


def prepare(count, part, first_col, factor_buf, inverse_buf, live_ref, flipped_ref, local_ref):
    def mask(a, _):
        rows = pl.multiple_of(a * BLOCK, BLOCK)
        value = factor_buf[part, pl.ds(rows, BLOCK), :]
        value = jnp.where(a < count, value, jnp.zeros_like(value))
        turned = value.T
        for lap in range(2):
            at = pl.multiple_of(rows + lap * NOV * BLOCK, BLOCK)
            live_ref[part, pl.ds(at, BLOCK), :] = value
            flipped_ref[part, :, pl.ds(at, BLOCK)] = turned
        return 0

    lax.fori_loop(0, NOV, mask, 0)

    def local(step, total):
        rows = pl.multiple_of(step * 512, 512)
        value = inverse_buf[part, pl.ds(rows, 512), :]
        row_at = rows + lax.broadcasted_iota(jnp.int32, value.shape, 0)
        col_at = first_col + lax.broadcasted_iota(jnp.int32, value.shape, 1)
        value = jnp.where(row_at >= col_at, value, jnp.zeros_like(value))
        return total + lax.dot_general(
            value, value, (((0,), (0,)), ((), ())), preferred_element_type=jnp.float32
        )

    local_ref[part] = lax.fori_loop(0, 8, local, jnp.zeros((256, 256), jnp.float32))


def gather_kernel(
    counts_ref, parent_ref, margin_ref, factor_ref, inverse_ref,
    out_ref, live_ref, flipped_ref, local_ref,
    parent_buf, factor_buf, inverse_buf, slabs, picked, margin_buf, margin_smem,
    t_send, t_recv, d_send, d_recv, m_send, m_recv, l_sem, x_send, x_recv, g_send, g_recv,
):
    front = lax.axis_index("front")
    row = lax.axis_index("row")
    x, core = front // 2, front % 2
    z, y = row // 4, row % 4
    half, yh = y % 2, y // 2
    fold = half * 2 + yh
    me_q = yh * 16 + z * 4 + x
    my_block = 16 * x + 8 * core + 2 * z + yh
    sibling = place(x, 1 - core, y, z)
    y_up = place(x, core, (y + 1) % 4, z)
    y_down = place(x, core, (y + 3) % 4, z)
    z_up = place(x, core, y, (z + 1) % 4)
    z_down = place(x, core, y, (z + 3) % 4)

    def member(q):
        return place(q % 4, core, 2 * (q // 16) + half, (q // 4) % 4)

    parent_load = pltpu.make_async_copy(parent_ref, parent_buf, l_sem.at[0])
    parent_load.start()
    factor_load = pltpu.make_async_copy(factor_ref, factor_buf, l_sem.at[1])
    factor_load.start()
    inverse_load = pltpu.make_async_copy(inverse_ref, inverse_buf, l_sem.at[2])
    inverse_load.start()

    barrier = pltpu.get_barrier_semaphore()

    def greet(step, _):
        pl.semaphore_signal(
            barrier, inc=1, device_id=member((me_q + step) % 32), device_id_type=MESH
        )
        return 0

    lax.fori_loop(1, 32, greet, 0)
    for other in (sibling, y_up, y_down):
        pl.semaphore_signal(barrier, inc=1, device_id=other, device_id_type=MESH)
    parent_load.wait()
    pl.semaphore_wait(barrier, 34)

    margin_sends = []
    for step in (1, 2, 3):
        copy = pltpu.make_async_remote_copy(
            src_ref=margin_ref,
            dst_ref=margin_buf.at[x],
            send_sem=m_send.at[step],
            recv_sem=m_recv.at[x],
            device_id=place((x + step) % 4, core, y, z),
            device_id_type=MESH,
        )
        copy.start()
        margin_sends.append(copy)
    pltpu.make_async_copy(margin_ref, margin_buf.at[x], m_recv.at[x]).start()
    pltpu.make_async_copy(
        parent_buf.at[me_q // 4, :, me_q % 4], slabs.at[my_block], t_recv.at[x]
    ).start()

    def spread(step, _):
        q = (me_q + step) % 32
        pltpu.make_async_remote_copy(
            src_ref=parent_buf.at[q // 4, :, q % 4],
            dst_ref=slabs.at[my_block],
            send_sem=t_send,
            recv_sem=t_recv.at[x],
            device_id=member(q),
            device_id_type=MESH,
        ).start()
        return 0

    lax.fori_loop(1, 32, spread, 0)

    for source in range(4):
        pltpu.make_async_copy(margin_ref, margin_buf.at[source], m_recv.at[source]).wait()
    to_smem = pltpu.make_async_copy(margin_buf, margin_smem, l_sem.at[3])
    to_smem.start()
    to_smem.wait()

    factor_load.wait()
    inverse_load.wait()
    for part in range(2):
        prepare(
            counts_ref[part], part, row * 256, factor_buf, inverse_buf,
            live_ref, flipped_ref, local_ref,
        )

    exchanges = []
    for source in range(4):
        group = slabs.at[pl.ds(16 * source + 8 * core, 8)]
        pltpu.make_async_copy(group, group, t_recv.at[source]).wait()
        copy = pltpu.make_async_remote_copy(
            src_ref=group,
            dst_ref=group,
            send_sem=d_send.at[source],
            recv_sem=d_recv.at[source],
            device_id=sibling,
            device_id_type=MESH,
        )
        copy.start()
        exchanges.append(copy)
    for copy in exchanges:
        copy.wait()

    def x_part(ref, chunk):
        return ref.at[:, pl.ds(chunk * ROWS, ROWS), pl.ds(0, band(chunk))]

    def landing(chunk):
        return out_ref.at[
            :, pl.ds(chunk * ROWS, ROWS), pl.ds(0, band(chunk)), fold, z, x
        ]

    x_copies = [[] for _ in range(CHUNKS)]
    for chunk in range(CHUNKS):
        for step in (2, 1, 3, 0):
            target = (x + step) % 4

            def pick(index, _):
                part, a = index // ROWS, chunk * ROWS + index % ROWS
                block_row = margin_smem[target, part, a]
                for d in range(band(chunk)):
                    block_col = margin_smem[target, part, (a + d) % NOV]
                    picked[target, part, a, d] = slabs[block_row, block_col]
                return 0

            lax.fori_loop(0, 2 * ROWS, pick, 0)
            slot = 4 * chunk + step
            if step:
                copy = pltpu.make_async_remote_copy(
                    src_ref=x_part(picked.at[target], chunk),
                    dst_ref=landing(chunk),
                    send_sem=x_send.at[slot],
                    recv_sem=x_recv.at[slot],
                    device_id=place(target, core, y, z),
                    device_id_type=MESH,
                )
            else:
                copy = pltpu.make_async_copy(
                    x_part(picked.at[target], chunk), landing(chunk), x_recv.at[slot]
                )
            copy.start()
            x_copies[chunk].append(copy)

    def first_piece(part, lo, size, chunk, at):
        rows, dists = pl.ds(lo, size), pl.ds(0, band(chunk))
        if part == 0:
            return out_ref.at[0, rows, dists, (at % 2) * 2 + at // 2, z]
        return out_ref.at[1, rows, dists, fold, at]

    def second_piece(part, lo, size, chunk, at):
        rows, dists = pl.ds(lo, size), pl.ds(0, band(chunk))
        if part == 0:
            return out_ref.at[0, rows, dists, :, at]
        return out_ref.at[1, rows, dists, (at % 2) * 2 + at // 2]

    sends = []

    def send(ref, slot, device):
        copy = pltpu.make_async_remote_copy(
            src_ref=ref, dst_ref=ref, send_sem=g_send.at[slot], recv_sem=g_recv.at[slot],
            device_id=device, device_id_type=MESH,
        )
        copy.start()
        sends.append(copy)

    def landed(ref, slot):
        pltpu.make_async_copy(ref, ref, g_recv.at[slot]).wait()

    def ring(part, phase):
        if part == phase:
            return y, y_up, y_down
        return z, z_up, z_down

    def base(part, phase, chunk):
        return 4 * (part + 2 * (phase + 2 * chunk))

    pieces = (first_piece, second_piece)
    mid = ROWS // 2

    def start_direct(phase, chunk):
        for part in range(2):
            here, up, down = ring(part, phase)
            own = pieces[phase](part, chunk * ROWS, ROWS, chunk, here)
            send(own, base(part, phase, chunk), up)
            send(own, base(part, phase, chunk) + 1, down)

    def forward(phase, chunk):
        for part in range(2):
            here, up, down = ring(part, phase)
            slot, lo = base(part, phase, chunk), chunk * ROWS
            below, above = (here + 3) % 4, (here + 1) % 4
            landed(pieces[phase](part, lo, ROWS, chunk, below), slot)
            send(pieces[phase](part, lo, mid, chunk, below), slot + 2, up)
            landed(pieces[phase](part, lo, ROWS, chunk, above), slot + 1)
            send(pieces[phase](part, lo + mid, ROWS - mid, chunk, above), slot + 3, down)

    def finish(phase, chunk):
        for part in range(2):
            here = ring(part, phase)[0]
            slot, lo, far = base(part, phase, chunk), chunk * ROWS, (here + 2) % 4
            landed(pieces[phase](part, lo, mid, chunk, far), slot + 2)
            landed(pieces[phase](part, lo + mid, ROWS - mid, chunk, far), slot + 3)

    for turn in range(CHUNKS + 4):
        if turn < CHUNKS:
            for copy in x_copies[turn]:
                copy.wait()
            start_direct(0, turn)
        if 0 <= turn - 1 < CHUNKS:
            forward(0, turn - 1)
        if 0 <= turn - 2 < CHUNKS:
            finish(0, turn - 2)
            start_direct(1, turn - 2)
        if 0 <= turn - 3 < CHUNKS:
            forward(1, turn - 3)
        if 0 <= turn - 4 < CHUNKS:
            finish(1, turn - 4)

    for copy in sends:
        copy.wait_send()
    for copy in margin_sends:
        copy.wait_send()
    sent = slabs.at[pl.ds(0, 31)]
    pltpu.make_async_copy(sent, sent, t_send).wait()


def gathered(parent, margin, counts, factor, local_inverse):
    grid = parent.reshape(8, 4, 2, 64, BLOCK).transpose(0, 3, 1, 2, 4)
    dma = pltpu.SemaphoreType.DMA
    vmem = pl.BlockSpec(memory_space=pltpu.VMEM)
    hbm = pl.BlockSpec(memory_space=pltpu.HBM)
    return pl.pallas_call(
        gather_kernel,
        out_shape=(
            jax.ShapeDtypeStruct((2, NOV, 9, 4, 4, 4, 2, BLOCK), jnp.bfloat16),
            jax.ShapeDtypeStruct((2, 4096, 256), jnp.bfloat16),
            jax.ShapeDtypeStruct((2, 256, 4096), jnp.bfloat16),
            jax.ShapeDtypeStruct((2, 256, 256), jnp.float32),
        ),
        in_specs=[pl.BlockSpec(memory_space=pltpu.SMEM), hbm, vmem, hbm, hbm],
        out_specs=(vmem,) * 4,
        scratch_shapes=[
            pltpu.VMEM(grid.shape, jnp.bfloat16),
            pltpu.VMEM(factor.shape, jnp.bfloat16),
            pltpu.VMEM(local_inverse.shape, jnp.bfloat16),
            pltpu.VMEM((64, 64, 2, BLOCK), jnp.bfloat16),
            pltpu.VMEM((4, 2, NOV, 9, 2, BLOCK), jnp.bfloat16),
            pltpu.VMEM((4, 2, NOV), jnp.int32),
            pltpu.SMEM((4, 2, NOV), jnp.int32),
            dma, dma((4,)), dma((4,)), dma((4,)), dma((4,)), dma((4,)), dma((4,)),
            dma((4 * CHUNKS,)), dma((4 * CHUNKS,)), dma((16 * CHUNKS,)), dma((16 * CHUNKS,)),
        ],
        compiler_params=pltpu.CompilerParams(
            collective_id=0, has_side_effects=True, vmem_limit_bytes=28 * 2**20
        ),
        cost_estimate=pl.CostEstimate(
            flops=2 * 10**9, bytes_accessed=20 * 2**20, transcendentals=0
        ),
    )(counts, grid, margin, factor, local_inverse)


def update_kernel(counts_ref, sub_ref, live_ref, flipped_ref, local_ref, coupling_ref, diag_ref):
    part = pl.program_id(0)
    count = counts_ref[part]

    def pair(index, total, late):
        a = 2 * index
        rows = pl.multiple_of(a * BLOCK, 2 * BLOCK)
        zero = jnp.zeros((BLOCK, BLOCK), jnp.bfloat16)
        wide = 8 if late else 9
        deep = 8 if late else 7

        def block(r, d):
            return sub_ref[part, (r + NOV) % NOV, d]

        direct = jnp.concatenate(
            [
                jnp.concatenate([block(a, d) for d in range(wide)] + [zero], axis=1),
                jnp.concatenate([zero] + [block(a + 1, d) for d in range(wide)], axis=1),
            ],
            axis=0,
        )
        result = jnp.dot(
            direct, live_ref[part, pl.ds(rows, (wide + 1) * BLOCK), :],
            preferred_element_type=jnp.float32,
        )
        mirrored = jnp.concatenate(
            [
                jnp.concatenate([block(a - d, d), block(a - d, d + 1) if d < deep else zero], axis=1)
                if d
                else jnp.concatenate([zero, block(a, 1)], axis=1)
                for d in range(deep, -1, -1)
            ],
            axis=0,
        )
        start = pl.multiple_of(rows + (NOV - deep) * BLOCK, BLOCK)
        turned = jnp.dot(
            flipped_ref[part, :, pl.ds(start, (deep + 1) * BLOCK)], mirrored,
            preferred_element_type=jnp.float32,
        )
        result = -(result + turned.T)
        block_at = a + lax.broadcasted_iota(jnp.int32, result.shape, 0) // BLOCK
        result = jnp.where(block_at < count, result, jnp.zeros_like(result)).astype(jnp.bfloat16)
        coupling_ref[0, pl.ds(rows, 2 * BLOCK), :] = result
        return total - jnp.dot(
            flipped_ref[part, :, pl.ds(rows, 2 * BLOCK)], result,
            preferred_element_type=jnp.float32,
        )

    total = local_ref[part]
    total = lax.fori_loop(0, 4, functools.partial(pair, late=False), total)
    total = lax.fori_loop(4, 8, functools.partial(pair, late=True), total)
    for c in range(2):
        at = slice(c * BLOCK, (c + 1) * BLOCK)
        diag_ref[0, c] = total[at, at]


def body(parent, margin, counts, factor, local_inverse):
    sub, live, flipped, local = gathered(parent, margin, counts, factor, local_inverse)
    vmem = pl.BlockSpec(memory_space=pltpu.VMEM)
    return pl.pallas_call(
        update_kernel,
        grid=(2,),
        out_shape=(
            jax.ShapeDtypeStruct(factor.shape, jnp.bfloat16),
            jax.ShapeDtypeStruct((2, 2, BLOCK, BLOCK), jnp.float32),
        ),
        in_specs=[pl.BlockSpec(memory_space=pltpu.SMEM), vmem, vmem, vmem, vmem],
        out_specs=(
            pl.BlockSpec((1, 2048, 256), lambda f: (f, 0, 0)),
            pl.BlockSpec((1, 2, BLOCK, BLOCK), lambda f: (f, 0, 0, 0)),
        ),
        compiler_params=pltpu.CompilerParams(vmem_limit_bytes=16 * 2**20),
        cost_estimate=pl.CostEstimate(
            flops=6 * 10**9, bytes_accessed=20 * 2**20, transcendentals=0
        ),
    )(counts, sub.reshape(2, NOV, 9, BLOCK, BLOCK), live, flipped, local)


def solution(mesh):
    placed = (
        P(("front", "row"), None),
        P("front", None),
        P("front"),
        P("front", None, "row"),
        P("front", None, "row"),
    )
    return jax.shard_map(
        body,
        mesh=mesh,
        in_specs=placed,
        out_specs=(P("front", None, "row"), P("front", "row", None, None)),
        check_vma=False,
    )
```

time: 122 us -> 107 us (0.88)
  Pallas kernels: 116 us -> 100 us
  local copies, waits for them, and re-layouts: 4.85 us -> 6.34 us
    pallas_call x1, Pallas kernels: 22.4 us -> 13.9 us  [body(): pl.pallas_call(update_kernel, grid=(2,), out_shape=(jax.ShapeDtypeStruct(...]
    pallas_call x1, Pallas kernels: 93.6 us -> 86.3 us  [gathered(): pl.pallas_call(gather_kernel, out_shape=(jax.ShapeDtypeStruct((2, NOV, 9,...]
    unnamed x10 -> x12, local copies, waits for them, and re-layouts: 4.85 us -> 6.34 us
where the time goes in v2:
time: 107 us
  Pallas kernels  100 us (93%)
  local copies, waits for them, and re-layouts  6.34 us (6%)
    pallas_call x1, Pallas kernels, gathered(): pl.pallas_call(gather_kernel, out_shape=(jax.ShapeDtypeStruct((2, NOV, 9,...  86.3 us
    pallas_call x1, Pallas kernels, body(): pl.pallas_call(update_kernel, grid=(2,), out_shape=(jax.ShapeDtypeStruct(...  13.9 us
    unnamed x12, local copies, waits for them, and re-layouts  6.34 us

profile of v2, /device:TPU:0, one launch (start us, length us, event | category | flops | bytes accessed | tf_op | source)
XLA Modules:
  0.0 107.2 jit_solution(6142153760734639030)
XLA Ops:
  0.6 0.0 copy-start.5
  0.6 0.0 copy-start
  0.7 2.2 %copy-done = bf16[2,4096,256]{2,1,0:T(8,128)(2,1)S(1)} copy-done((bf16[2,4096,256]{2,1,0:T(8,128)(2,1)S(1)}, bf16[2,4096,256]{2,1,0:T(8,128)(2,1)}, u32[]{:S(2)}) %copy-start) | copy-done | bytes 4194328
  2.8 0.0 copy-start.1
  2.8 1.6 %copy-done.1 = bf16[2,2048,256]{2,1,0:T(8,128)(2,1)S(1)} copy-done((bf16[2,2048,256]{2,1,0:T(8,128)(2,1)S(1)}, bf16[2,2048,256]{2,1,0:T(8,128)(2,1)}, u32[]{:S(2)}) %copy-start.1) | copy-done | bytes 2097176
  4.4 0.0 copy-start.2
  4.4 1.2 %copy-done.2 = bf16[64,8192]{1,0:T(8,128)(2,1)S(1)} copy-done((bf16[64,8192]{1,0:T(8,128)(2,1)S(1)}, bf16[64,8192]{1,0:T(8,128)(2,1)}, u32[]{:S(2)}) %copy-start.2) | copy-done | bytes 1048600
  5.7 0.0 copy-start.3
  5.7 0.7 copy-done.3
  6.3 0.0 copy-start.4
  6.3 0.7 copy-done.4
  7.0 86.3 %shard_map.68 = (bf16[2,16,9,4,4,4,2,128]{7,6,5,4,3,2,1,0:T(2,128)(2,1)S(1)}, bf16[2,4096,256]{2,1,0:T(8,128)(2,1)S(1)}, bf16[2,256,4096]{2,1,0:T(8,128)(2,1)S(1)}, f32[2,256,256]{2,1,0:T(8,128)S(1)}) custom-call(s32[2]{0:T(128)S(1)} %copy-done.4, bf16[8,64,4,2,128]{4,3,2,1,0:T(2,128)(2,1)S(1)} %bitcast.4, s32[2,16]{1,0:T(2,128)S(1)} %copy-done.3, ...), custom_call_target="tpu_custom_call" | custom-call | flops 2000000000 | bytes 20971520 | tf_op jit(solution)/shard_map/pallas_call | solution.py:285
  93.3 0.0 copy-done.5
  93.3 13.9 %shard_map.69 = (bf16[2,2048,256]{2,1,0:T(8,128)(2,1)}, f32[2,2,128,128]{3,2,1,0:T(8,128)}) custom-call(s32[2]{0:T(128)S(1)} %copy-done.5, bf16[2,16,9,128,128]{4,3,2,1,0:T(8,128)(2,1)S(1)} %bitcast.5, bf16[2,4096,256]{2,1,0:T(8,128)(2,1)S(1)} %get-tuple-element.7.live_ref, bf16[2,256,4096]{2,1,0:T(8,128)(2,1)S(1)} %get-tuple-element.8.flipped_ref, ...), custom_call_target="tpu_custom_call" | custom-call | flops 6000000000 | bytes 20971520 | tf_op jit(solution)/shard_map/pallas_call | solution.py:374
Async XLA Ops:
  0.6 92.7 %copy-start.5 = (s32[2]{0:T(128)S(1)}, s32[2]{0:T(128)}, u32[]{:S(2)}) copy-start(s32[2]{0:T(128)} %counts_ref.3) | copy-start | bytes 28
  0.6 2.2 %copy-start = (bf16[2,4096,256]{2,1,0:T(8,128)(2,1)S(1)}, bf16[2,4096,256]{2,1,0:T(8,128)(2,1)}, u32[]{:S(2)}) copy-start(bf16[2,4096,256]{2,1,0:T(8,128)(2,1)} %inverse_ref.1) | copy-start | bytes 12582916
  2.8 1.6 %copy-start.1 = (bf16[2,2048,256]{2,1,0:T(8,128)(2,1)S(1)}, bf16[2,2048,256]{2,1,0:T(8,128)(2,1)}, u32[]{:S(2)}) copy-start(bf16[2,2048,256]{2,1,0:T(8,128)(2,1)} %factor_ref.1) | copy-start | bytes 6291460
  4.4 1.2 %copy-start.2 = (bf16[64,8192]{1,0:T(8,128)(2,1)S(1)}, bf16[64,8192]{1,0:T(8,128)(2,1)}, u32[]{:S(2)}) copy-start(bf16[64,8192]{1,0:T(8,128)(2,1)} %param.5) | copy-start | bytes 3145732
  5.7 0.7 copy-start.3
  6.3 0.7 copy-start.4

commit v3 on v2

--- a/solution.py
+++ b/solution.py
@@ -11,6 +11,7 @@
 NOV = 16
 BLOCK = 128
 CHUNKS = 4
+SLOTS = 20
 ROWS = NOV // CHUNKS
 
 
@@ -52,7 +53,7 @@
 def gather_kernel(
     counts_ref, parent_ref, margin_ref, factor_ref, inverse_ref,
     out_ref, live_ref, flipped_ref, local_ref,
-    parent_buf, factor_buf, inverse_buf, slabs, picked, margin_buf, margin_smem,
+    parent_buf, factor_buf, inverse_buf, slabs, picked, margin_buf, margin_smem, counts_smem,
     t_send, t_recv, d_send, d_recv, m_send, m_recv, l_sem, x_send, x_recv, g_send, g_recv,
 ):
     front = lax.axis_index("front")
@@ -78,6 +79,8 @@
     factor_load.start()
     inverse_load = pltpu.make_async_copy(inverse_ref, inverse_buf, l_sem.at[2])
     inverse_load.start()
+    counts_load = pltpu.make_async_copy(counts_ref, counts_smem, l_sem.at[4])
+    counts_load.start()
 
     barrier = pltpu.get_barrier_semaphore()
 
@@ -110,19 +113,21 @@
         parent_buf.at[me_q // 4, :, me_q % 4], slabs.at[my_block], t_recv.at[x]
     ).start()
 
-    def spread(step, _):
-        q = (me_q + step) % 32
-        pltpu.make_async_remote_copy(
-            src_ref=parent_buf.at[q // 4, :, q % 4],
-            dst_ref=slabs.at[my_block],
-            send_sem=t_send,
-            recv_sem=t_recv.at[x],
-            device_id=member(q),
-            device_id_type=MESH,
-        ).start()
-        return 0
-
-    lax.fori_loop(1, 32, spread, 0)
+    for offset in (0, 1, 3, 2):
+
+        def spread(step, _):
+            q = (yh * 4 + z + step) % 8 * 4 + (x + offset) % 4
+            pltpu.make_async_remote_copy(
+                src_ref=parent_buf.at[q // 4, :, q % 4],
+                dst_ref=slabs.at[my_block],
+                send_sem=t_send,
+                recv_sem=t_recv.at[x],
+                device_id=member(q),
+                device_id_type=MESH,
+            ).start()
+            return 0
+
+        lax.fori_loop(0 if offset else 1, 8, spread, 0)
 
     for source in range(4):
         pltpu.make_async_copy(margin_ref, margin_buf.at[source], m_recv.at[source]).wait()
@@ -132,14 +137,16 @@
 
     factor_load.wait()
     inverse_load.wait()
+    counts_load.wait()
     for part in range(2):
         prepare(
-            counts_ref[part], part, row * 256, factor_buf, inverse_buf,
+            counts_smem[part], part, row * 256, factor_buf, inverse_buf,
             live_ref, flipped_ref, local_ref,
         )
 
     exchanges = []
-    for source in range(4):
+    for offset in (0, 1, 3, 2):
+        source = (x + 4 - offset) % 4
         group = slabs.at[pl.ds(16 * source + 8 * core, 8)]
         pltpu.make_async_copy(group, group, t_recv.at[source]).wait()
         copy = pltpu.make_async_remote_copy(
@@ -164,7 +171,8 @@
         ]
 
     x_copies = [[] for _ in range(CHUNKS)]
-    for chunk in range(CHUNKS):
+
+    def start_x(chunk):
         for step in (2, 1, 3, 0):
             target = (x + step) % 4
 
@@ -194,80 +202,114 @@
             copy.start()
             x_copies[chunk].append(copy)
 
-    def first_piece(part, lo, size, chunk, at):
-        rows, dists = pl.ds(lo, size), pl.ds(0, band(chunk))
-        if part == 0:
-            return out_ref.at[0, rows, dists, (at % 2) * 2 + at // 2, z]
-        return out_ref.at[1, rows, dists, fold, at]
-
-    def second_piece(part, lo, size, chunk, at):
-        rows, dists = pl.ds(lo, size), pl.ds(0, band(chunk))
-        if part == 0:
-            return out_ref.at[0, rows, dists, :, at]
-        return out_ref.at[1, rows, dists, (at % 2) * 2 + at // 2]
-
+    first_axis = ((y, y_up, y_down), (z, z_up, z_down))
     sends = []
 
-    def send(ref, slot, device):
+    def piece(part, chunk, first_at, second_at, lo=0, size=ROWS):
+        y_at, z_at = (first_at, second_at) if part == 0 else (second_at, first_at)
+        return out_ref.at[
+            part, pl.ds(chunk * ROWS + lo, size), pl.ds(0, band(chunk)),
+            (y_at % 2) * 2 + y_at // 2, z_at,
+        ]
+
+    def sem_at(part, chunk, slot):
+        return SLOTS * (part + 2 * chunk) + slot
+
+    def send(part, chunk, slot, ref, device):
+        at = sem_at(part, chunk, slot)
         copy = pltpu.make_async_remote_copy(
-            src_ref=ref, dst_ref=ref, send_sem=g_send.at[slot], recv_sem=g_recv.at[slot],
+            src_ref=ref, dst_ref=ref, send_sem=g_send.at[at], recv_sem=g_recv.at[at],
             device_id=device, device_id_type=MESH,
         )
         copy.start()
         sends.append(copy)
 
-    def landed(ref, slot):
-        pltpu.make_async_copy(ref, ref, g_recv.at[slot]).wait()
-
-    def ring(part, phase):
-        if part == phase:
-            return y, y_up, y_down
-        return z, z_up, z_down
-
-    def base(part, phase, chunk):
-        return 4 * (part + 2 * (phase + 2 * chunk))
-
-    pieces = (first_piece, second_piece)
+    def landed(part, chunk, slot, ref):
+        pltpu.make_async_copy(ref, ref, g_recv.at[sem_at(part, chunk, slot)]).wait()
+
     mid = ROWS // 2
 
-    def start_direct(phase, chunk):
-        for part in range(2):
-            here, up, down = ring(part, phase)
-            own = pieces[phase](part, chunk * ROWS, ROWS, chunk, here)
-            send(own, base(part, phase, chunk), up)
-            send(own, base(part, phase, chunk) + 1, down)
-
-    def forward(phase, chunk):
-        for part in range(2):
-            here, up, down = ring(part, phase)
-            slot, lo = base(part, phase, chunk), chunk * ROWS
-            below, above = (here + 3) % 4, (here + 1) % 4
-            landed(pieces[phase](part, lo, ROWS, chunk, below), slot)
-            send(pieces[phase](part, lo, mid, chunk, below), slot + 2, up)
-            landed(pieces[phase](part, lo, ROWS, chunk, above), slot + 1)
-            send(pieces[phase](part, lo + mid, ROWS - mid, chunk, above), slot + 3, down)
-
-    def finish(phase, chunk):
-        for part in range(2):
-            here = ring(part, phase)[0]
-            slot, lo, far = base(part, phase, chunk), chunk * ROWS, (here + 2) % 4
-            landed(pieces[phase](part, lo, mid, chunk, far), slot + 2)
-            landed(pieces[phase](part, lo + mid, ROWS - mid, chunk, far), slot + 3)
-
+    def send_both(part, chunk, slot, ref, ring):
+        send(part, chunk, slot, ref, ring[1])
+        send(part, chunk, slot + 1, ref, ring[2])
+
+    def pass_on(part, chunk, slot, below, above, ring, get):
+        landed(part, chunk, slot, get(below, 0, ROWS))
+        send(part, chunk, slot + 2, get(below, 0, mid), ring[1])
+        landed(part, chunk, slot + 1, get(above, 0, ROWS))
+        send(part, chunk, slot + 3, get(above, mid, ROWS - mid), ring[2])
+
+    def second_direct(part, chunk, number, first_at):
+        other = first_axis[1 - part]
+        send_both(part, chunk, 4 + 4 * number, piece(part, chunk, first_at, other[0]), other)
+
+    def second_forward(part, chunk, number, first_at):
+        other = first_axis[1 - part]
+        at = other[0]
+        pass_on(
+            part, chunk, 4 + 4 * number, (at + 3) % 4, (at + 1) % 4, other,
+            lambda second_at, lo, size: piece(part, chunk, first_at, second_at, lo, size),
+        )
+
+    def step_own(chunk):
+        for copy in x_copies[chunk]:
+            copy.wait()
+        for part in range(2):
+            ring, other = first_axis[part], first_axis[1 - part]
+            own = piece(part, chunk, ring[0], other[0])
+            send_both(part, chunk, 0, own, ring)
+        for part in range(2):
+            second_direct(part, chunk, 0, first_axis[part][0])
+
+    def step_near(chunk):
+        for part in range(2):
+            ring, other = first_axis[part], first_axis[1 - part]
+            here = ring[0]
+            pass_on(
+                part, chunk, 0, (here + 3) % 4, (here + 1) % 4, ring,
+                lambda first_at, lo, size: piece(part, chunk, first_at, other[0], lo, size),
+            )
+        for part in range(2):
+            here = first_axis[part][0]
+            second_direct(part, chunk, 1, (here + 3) % 4)
+            second_direct(part, chunk, 2, (here + 1) % 4)
+        for part in range(2):
+            second_forward(part, chunk, 0, first_axis[part][0])
+
+    def step_far(chunk):
+        for part in range(2):
+            ring, other = first_axis[part], first_axis[1 - part]
+            far = (ring[0] + 2) % 4
+            landed(part, chunk, 2, piece(part, chunk, far, other[0], 0, mid))
+            landed(part, chunk, 3, piece(part, chunk, far, other[0], mid, ROWS - mid))
+            second_direct(part, chunk, 3, far)
+        for part in range(2):
+            here = first_axis[part][0]
+            second_forward(part, chunk, 1, (here + 3) % 4)
+            second_forward(part, chunk, 2, (here + 1) % 4)
+
+    def step_last(chunk):
+        for part in range(2):
+            second_forward(part, chunk, 3, (first_axis[part][0] + 2) % 4)
+
+    def step_end(chunk):
+        for part in range(2):
+            here, far = first_axis[part][0], (first_axis[1 - part][0] + 2) % 4
+            for number, first_at in enumerate((here, (here + 3) % 4, (here + 1) % 4, (here + 2) % 4)):
+                landed(part, chunk, 6 + 4 * number, piece(part, chunk, first_at, far, 0, mid))
+                landed(
+                    part, chunk, 7 + 4 * number,
+                    piece(part, chunk, first_at, far, mid, ROWS - mid),
+                )
+
+    start_x(0)
+    start_x(1)
     for turn in range(CHUNKS + 4):
-        if turn < CHUNKS:
-            for copy in x_copies[turn]:
-                copy.wait()
-            start_direct(0, turn)
-        if 0 <= turn - 1 < CHUNKS:
-            forward(0, turn - 1)
-        if 0 <= turn - 2 < CHUNKS:
-            finish(0, turn - 2)
-            start_direct(1, turn - 2)
-        if 0 <= turn - 3 < CHUNKS:
-            forward(1, turn - 3)
-        if 0 <= turn - 4 < CHUNKS:
-            finish(1, turn - 4)
+        for delay, step in enumerate((step_own, step_near, step_far, step_last, step_end)):
+            if 0 <= turn - delay < CHUNKS:
+                step(turn - delay)
+                if delay == 0 and turn + 2 < CHUNKS:
+                    start_x(turn + 2)
 
     for copy in sends:
         copy.wait_send()
@@ -290,7 +332,7 @@
             jax.ShapeDtypeStruct((2, 256, 4096), jnp.bfloat16),
             jax.ShapeDtypeStruct((2, 256, 256), jnp.float32),
         ),
-        in_specs=[pl.BlockSpec(memory_space=pltpu.SMEM), hbm, vmem, hbm, hbm],
+        in_specs=[hbm] * 5,
         out_specs=(vmem,) * 4,
         scratch_shapes=[
             pltpu.VMEM(grid.shape, jnp.bfloat16),
@@ -300,8 +342,10 @@
             pltpu.VMEM((4, 2, NOV, 9, 2, BLOCK), jnp.bfloat16),
             pltpu.VMEM((4, 2, NOV), jnp.int32),
             pltpu.SMEM((4, 2, NOV), jnp.int32),
-            dma, dma((4,)), dma((4,)), dma((4,)), dma((4,)), dma((4,)), dma((4,)),
-            dma((4 * CHUNKS,)), dma((4 * CHUNKS,)), dma((16 * CHUNKS,)), dma((16 * CHUNKS,)),
+            pltpu.SMEM((2,), jnp.int32),
+            dma, dma((4,)), dma((4,)), dma((4,)), dma((4,)), dma((4,)), dma((5,)),
+            dma((4 * CHUNKS,)), dma((4 * CHUNKS,)),
+            dma((2 * SLOTS * CHUNKS,)), dma((2 * SLOTS * CHUNKS,)),
         ],
         compiler_params=pltpu.CompilerParams(
             collective_id=0, has_side_effects=True, vmem_limit_bytes=28 * 2**20
@@ -309,7 +353,10 @@
         cost_estimate=pl.CostEstimate(
             flops=2 * 10**9, bytes_accessed=20 * 2**20, transcendentals=0
         ),
-    )(counts, grid, margin, factor, local_inverse)
+    )(*[
+        pltpu.with_memory_space_constraint(value, pltpu.HBM)
+        for value in (counts, grid, margin, factor, local_inverse)
+    ])
 
 
 def update_kernel(counts_ref, sub_ref, live_ref, flipped_ref, local_ref, coupling_ref, diag_ref):
@@ -361,8 +408,8 @@
         )
 
     total = local_ref[part]
-    total = lax.fori_loop(0, 4, functools.partial(pair, late=False), total)
-    total = lax.fori_loop(4, 8, functools.partial(pair, late=True), total)
+    total = lax.fori_loop(0, 4, functools.partial(pair, late=False), total, unroll=4)
+    total = lax.fori_loop(4, 8, functools.partial(pair, late=True), total, unroll=4)
     for c in range(2):
         at = slice(c * BLOCK, (c + 1) * BLOCK)
         diag_ref[0, c] = total[at, at]

time: 107 us -> 95.6 us (0.89)
  local copies, waits for them, and re-layouts: 6.34 us -> 0.01 us
  Pallas kernels: 100 us -> 94.8 us
    unnamed x12 -> x2, local copies, waits for them, and re-layouts: 6.34 us -> 0.01 us
    pallas_call x1, Pallas kernels: 13.9 us -> 10.8 us  [body(): pl.pallas_call(update_kernel, grid=(2,), out_shape=(jax.ShapeDtypeStruct(...]
    pallas_call x1, Pallas kernels: 86.3 us -> 84 us  [gathered(): pl.pallas_call(gather_kernel, out_shape=(jax.ShapeDtypeStruct((2, NOV, 9,...]
where the time goes in v3:
time: 95.6 us; the launch traced here: 95.5 us
  Pallas kernels  94.8 us (99%)
    pallas_call x1, Pallas kernels, gathered(): pl.pallas_call(gather_kernel, out_shape=(jax.ShapeDtypeStruct((2, NOV, 9,...  84 us
    pallas_call x1, Pallas kernels, body(): pl.pallas_call(update_kernel, grid=(2,), out_shape=(jax.ShapeDtypeStruct(...  10.8 us

profile of v3, /device:TPU:0, one launch (start us, length us, event | category | flops | bytes accessed | tf_op | source)
XLA Modules:
  0.0 95.5 jit_solution(1071262243378833321)
XLA Ops:
  0.6 0.0 copy-start
  0.6 84.0 %shard_map.68 = (bf16[2,16,9,4,4,4,2,128]{7,6,5,4,3,2,1,0:T(2,128)(2,1)S(1)}, bf16[2,4096,256]{2,1,0:T(8,128)(2,1)S(1)}, bf16[2,256,4096]{2,1,0:T(8,128)(2,1)S(1)}, f32[2,256,256]{2,1,0:T(8,128)S(1)}) custom-call(s32[2]{0:T(128)} %counts_ref.3, bf16[8,64,4,2,128]{4,3,2,1,0:T(2,128)(2,1)} %bitcast.5, s32[2,16]{1,0:T(2,128)} %margin_ref.1, ...), custom_call_target="tpu_custom_call" | custom-call | flops 2000000000 | bytes 20971520 | tf_op jit(solution)/shard_map/pallas_call | solution.py:327
  84.7 0.0 copy-done
  84.7 10.8 %shard_map.69 = (bf16[2,2048,256]{2,1,0:T(8,128)(2,1)}, f32[2,2,128,128]{3,2,1,0:T(8,128)}) custom-call(s32[2]{0:T(128)S(1)} %copy-done, bf16[2,16,9,128,128]{4,3,2,1,0:T(8,128)(2,1)S(1)} %bitcast.4, bf16[2,4096,256]{2,1,0:T(8,128)(2,1)S(1)} %get-tuple-element.7.live_ref, bf16[2,256,4096]{2,1,0:T(8,128)(2,1)S(1)} %get-tuple-element.8.flipped_ref, ...), custom_call_target="tpu_custom_call" | custom-call | flops 6000000000 | bytes 20971520 | tf_op jit(solution)/shard_map/pallas_call | solution.py:421
Async XLA Ops:
  0.6 84.0 %copy-start = (s32[2]{0:T(128)S(1)}, s32[2]{0:T(128)}, u32[]{:S(2)}) copy-start(s32[2]{0:T(128)} %counts_ref.3) | copy-start | bytes 28

commit v4 on v3

v4 whole, which is shorter than its diff:
```python
import functools

import jax
import jax.numpy as jnp
from jax import lax
from jax.experimental import pallas as pl
from jax.experimental.pallas import tpu as pltpu
from jax.sharding import PartitionSpec as P

MESH = pl.DeviceIdType.MESH
NOV = 16
BLOCK = 128
CHUNKS = 4
SLOTS = 20
ROWS = NOV // CHUNKS


def place(x, core, y, z):
    return (2 * x + core, 4 * z + y)


def band(chunk):
    return 9 if chunk < CHUNKS // 2 else 8


def partners(x, core, y, z, up):
    return place(x, core, (y + up * (1 - core)) % 4, (z + up * core) % 4)


def others(x, core, y, z, up):
    return place(x, core, (y + up * core) % 4, (z + up * (1 - core)) % 4)


def prepare_factor(count, part, factor_buf, lent_buf, live_ref, flipped_ref):
    def mask(a, _):
        rows = pl.multiple_of(a * BLOCK, BLOCK)
        value = jnp.concatenate(
            [
                factor_buf[part, pl.ds(rows, BLOCK), :],
                lent_buf[0, pl.ds(rows, BLOCK), :],
                lent_buf[1, pl.ds(rows, BLOCK), :],
            ],
            axis=1,
        )
        value = jnp.where(a < count, value, jnp.zeros_like(value))
        turned = value.T
        for lap in range(2):
            at = pl.multiple_of(rows + lap * NOV * BLOCK, BLOCK)
            live_ref[pl.ds(at, BLOCK), :] = value
            flipped_ref[:, pl.ds(at, BLOCK)] = turned
        return 0

    lax.fori_loop(0, NOV, mask, 0)


def prepare_local(part, first_col, inverse_buf, local_ref):
    def local(step, total):
        rows = pl.multiple_of(step * 512, 512)
        value = inverse_buf[part, pl.ds(rows, 512), :]
        row_at = rows + lax.broadcasted_iota(jnp.int32, value.shape, 0)
        col_at = first_col + lax.broadcasted_iota(jnp.int32, value.shape, 1)
        value = jnp.where(row_at >= col_at, value, jnp.zeros_like(value))
        return total + lax.dot_general(
            value, value, (((0,), (0,)), ((), ())), preferred_element_type=jnp.float32
        )

    local_ref[part] = lax.fori_loop(0, 8, local, jnp.zeros((256, 256), jnp.float32))


def gather_kernel(
    counts_ref, parent_ref, margin_ref, factor_ref, inverse_ref,
    out_ref, live_ref, flipped_ref, local_ref,
    parent_buf, factor_buf, inverse_buf, lent_buf, other_buf, slabs, picked, margin_buf, margin_smem, counts_smem,
    t_send, t_recv, d_send, d_recv, m_send, m_recv, l_sem, f_send, f_recv, x_send, x_recv, g_send, g_recv,
):
    front = lax.axis_index("front")
    row = lax.axis_index("row")
    x, core = front // 2, front % 2
    z, y = row // 4, row % 4
    half, yh = y % 2, y // 2
    fold = half * 2 + yh
    me_q = yh * 16 + z * 4 + x
    my_block = 16 * x + 8 * core + 2 * z + yh
    here = y * (1 - core) + z * core
    there = z * (1 - core) + y * core
    mine = here % 2
    sibling = place(x, 1 - core, y, z)
    pair_up = partners(x, core, y, z, 1)
    pair_down = partners(x, core, y, z, 3)
    pair_far = partners(x, core, y, z, 2)
    ring_up = others(x, core, y, z, 1)
    ring_down = others(x, core, y, z, 3)
    y_up = place(x, core, (y + 1) % 4, z)
    y_down = place(x, core, (y + 3) % 4, z)

    def member(q):
        return place(q % 4, core, 2 * (q // 16) + half, (q // 4) % 4)

    parent_load = pltpu.make_async_copy(parent_ref, parent_buf, l_sem.at[0])
    parent_load.start()
    factor_load = pltpu.make_async_copy(factor_ref, factor_buf, l_sem.at[1])
    factor_load.start()
    inverse_load = pltpu.make_async_copy(inverse_ref, inverse_buf, l_sem.at[2])
    inverse_load.start()
    counts_load = pltpu.make_async_copy(counts_ref, counts_smem, l_sem.at[4])
    counts_load.start()

    barrier = pltpu.get_barrier_semaphore()

    def greet(step, _):
        pl.semaphore_signal(
            barrier, inc=1, device_id=member((me_q + step) % 32), device_id_type=MESH
        )
        return 0

    lax.fori_loop(1, 32, greet, 0)
    for other in (sibling, y_up, y_down):
        pl.semaphore_signal(barrier, inc=1, device_id=other, device_id_type=MESH)
    parent_load.wait()
    pl.semaphore_wait(barrier, 34)

    margin_sends = []
    for step in (1, 2, 3):
        copy = pltpu.make_async_remote_copy(
            src_ref=margin_ref,
            dst_ref=margin_buf.at[x],
            send_sem=m_send.at[step],
            recv_sem=m_recv.at[x],
            device_id=place((x + step) % 4, core, y, z),
            device_id_type=MESH,
        )
        copy.start()
        margin_sends.append(copy)
    pltpu.make_async_copy(margin_ref, margin_buf.at[x], m_recv.at[x]).start()
    pltpu.make_async_copy(
        parent_buf.at[me_q // 4, :, me_q % 4], slabs.at[my_block], t_recv.at[x]
    ).start()

    for offset in (0, 1, 3, 2):

        def spread(step, _):
            q = (yh * 4 + z + step) % 8 * 4 + (x + offset) % 4
            pltpu.make_async_remote_copy(
                src_ref=parent_buf.at[q // 4, :, q % 4],
                dst_ref=slabs.at[my_block],
                send_sem=t_send,
                recv_sem=t_recv.at[x],
                device_id=member(q),
                device_id_type=MESH,
            ).start()
            return 0

        lax.fori_loop(0 if offset else 1, 8, spread, 0)

    for source in range(4):
        pltpu.make_async_copy(margin_ref, margin_buf.at[source], m_recv.at[source]).wait()
    to_smem = pltpu.make_async_copy(margin_buf, margin_smem, l_sem.at[3])
    to_smem.start()
    to_smem.wait()

    exchanges = []
    for offset in (0, 1, 3, 2):
        source = (x + 4 - offset) % 4
        group = slabs.at[pl.ds(16 * source + 8 * core, 8)]
        pltpu.make_async_copy(group, group, t_recv.at[source]).wait()
        copy = pltpu.make_async_remote_copy(
            src_ref=group,
            dst_ref=group,
            send_sem=d_send.at[source],
            recv_sem=d_recv.at[source],
            device_id=sibling,
            device_id_type=MESH,
        )
        copy.start()
        exchanges.append(copy)

    factor_load.wait()
    lends = []
    for number, device in enumerate((pair_up, pair_down)):
        copy = pltpu.make_async_remote_copy(
            src_ref=factor_buf.at[1 - mine, :, pl.ds(number * BLOCK, BLOCK)],
            dst_ref=lent_buf.at[number],
            send_sem=f_send.at[number],
            recv_sem=f_recv.at[number],
            device_id=device,
            device_id_type=MESH,
        )
        copy.start()
        lends.append(copy)

    for copy in exchanges:
        copy.wait()

    def span(chunk):
        return pl.ds(chunk * ROWS, ROWS), pl.ds(0, band(chunk))

    x_copies = [[] for _ in range(CHUNKS)]

    def start_x(chunk):
        rows, dists = span(chunk)
        for step in (2, 1, 3, 0):
            target = (x + step) % 4

            def pick(index, _):
                part, a = index // ROWS, chunk * ROWS + index % ROWS
                block_row = margin_smem[target, part, a]
                for d in range(band(chunk)):
                    block_col = margin_smem[target, part, (a + d) % NOV]
                    picked[target, part, a, d] = slabs[block_row, block_col]
                return 0

            lax.fori_loop(0, 2 * ROWS, pick, 0)
            slot = 8 * chunk + 2 * step
            lands = (out_ref.at[rows, dists, fold, z, x], other_buf.at[rows, dists, x])
            for number, land in enumerate(lands):
                part = (mine + number) % 2
                if step:
                    copy = pltpu.make_async_remote_copy(
                        src_ref=picked.at[target, part, rows, dists],
                        dst_ref=land,
                        send_sem=x_send.at[slot + number],
                        recv_sem=x_recv.at[slot + number],
                        device_id=place(target, core, y, z),
                        device_id_type=MESH,
                    )
                else:
                    copy = pltpu.make_async_copy(
                        picked.at[target, part, rows, dists], land, x_recv.at[slot + number]
                    )
                copy.start()
                x_copies[chunk].append(copy)

    sends = []

    def piece(chunk, pair_at, ring_at, lo=0, size=ROWS):
        y_at = pair_at * (1 - core) + ring_at * core
        z_at = ring_at * (1 - core) + pair_at * core
        return out_ref.at[
            pl.ds(chunk * ROWS + lo, size), pl.ds(0, band(chunk)),
            (y_at % 2) * 2 + y_at // 2, z_at,
        ]

    def send(chunk, slot, source, target, device):
        at = SLOTS * chunk + slot
        copy = pltpu.make_async_remote_copy(
            src_ref=source, dst_ref=target, send_sem=g_send.at[at], recv_sem=g_recv.at[at],
            device_id=device, device_id_type=MESH,
        )
        copy.start()
        sends.append(copy)

    def landed(chunk, slot, ref):
        pltpu.make_async_copy(ref, ref, g_recv.at[SLOTS * chunk + slot]).wait()

    mid = ROWS // 2
    pair_places = (here, (here + 3) % 4, (here + 1) % 4, (here + 2) % 4)
    above, below, far = (there + 1) % 4, (there + 3) % 4, (there + 2) % 4

    def ring_direct(chunk, number):
        own = piece(chunk, pair_places[number], there)
        send(chunk, 4 + 4 * number, own, own, ring_up)
        send(chunk, 5 + 4 * number, own, own, ring_down)

    def ring_forward(chunk, number):
        at = pair_places[number]
        landed(chunk, 4 + 4 * number, piece(chunk, at, below))
        low = piece(chunk, at, below, 0, mid)
        send(chunk, 6 + 4 * number, low, low, ring_up)
        landed(chunk, 5 + 4 * number, piece(chunk, at, above))
        high = piece(chunk, at, above, mid, ROWS - mid)
        send(chunk, 7 + 4 * number, high, high, ring_down)

    def step_own(chunk):
        rows, dists = span(chunk)
        for copy in x_copies[chunk]:
            copy.wait()
        own = piece(chunk, here, there)
        other = other_buf.at[rows, dists]
        send(chunk, 0, other, own, pair_up)
        send(chunk, 1, other, own, pair_down)
        send(chunk, 2, own, own, pair_far)
        ring_direct(chunk, 0)

    def step_near(chunk):
        for number in (1, 2, 3):
            landed(chunk, number - 1, piece(chunk, pair_places[number], there))
            ring_direct(chunk, number)
        ring_forward(chunk, 0)

    def step_far(chunk):
        for number in (1, 2, 3):
            ring_forward(chunk, number)

    def step_end(chunk):
        for number, at in enumerate(pair_places):
            landed(chunk, 6 + 4 * number, piece(chunk, at, far, 0, mid))
            landed(chunk, 7 + 4 * number, piece(chunk, at, far, mid, ROWS - mid))

    start_x(0)
    start_x(1)
    for turn in range(CHUNKS + 3):
        for delay, step in enumerate((step_own, step_near, step_far, step_end)):
            if 0 <= turn - delay < CHUNKS:
                step(turn - delay)
                if delay == 0 and turn + 2 < CHUNKS:
                    start_x(turn + 2)
        if turn == 1:
            for copy in lends:
                copy.wait()
            counts_load.wait()
            prepare_factor(counts_smem[mine], mine, factor_buf, lent_buf, live_ref, flipped_ref)
        if turn == 2:
            inverse_load.wait()
            for part in range(2):
                prepare_local(part, row * 256, inverse_buf, local_ref)

    for copy in sends:
        copy.wait_send()
    for copy in margin_sends:
        copy.wait_send()
    sent = slabs.at[pl.ds(0, 31)]
    pltpu.make_async_copy(sent, sent, t_send).wait()


def gathered(parent, margin, counts, factor, local_inverse):
    grid = parent.reshape(8, 4, 2, 64, BLOCK).transpose(0, 3, 1, 2, 4)
    dma = pltpu.SemaphoreType.DMA
    vmem = pl.BlockSpec(memory_space=pltpu.VMEM)
    hbm = pl.BlockSpec(memory_space=pltpu.HBM)
    return pl.pallas_call(
        gather_kernel,
        out_shape=(
            jax.ShapeDtypeStruct((NOV, 9, 4, 4, 4, 2, BLOCK), jnp.bfloat16),
            jax.ShapeDtypeStruct((4096, 512), jnp.bfloat16),
            jax.ShapeDtypeStruct((512, 4096), jnp.bfloat16),
            jax.ShapeDtypeStruct((2, 256, 256), jnp.float32),
        ),
        in_specs=[hbm] * 5,
        out_specs=(vmem,) * 4,
        scratch_shapes=[
            pltpu.VMEM(grid.shape, jnp.bfloat16),
            pltpu.VMEM(factor.shape, jnp.bfloat16),
            pltpu.VMEM(local_inverse.shape, jnp.bfloat16),
            pltpu.VMEM((2, 2048, BLOCK), jnp.bfloat16),
            pltpu.VMEM((NOV, 9, 4, 2, BLOCK), jnp.bfloat16),
            pltpu.VMEM((64, 64, 2, BLOCK), jnp.bfloat16),
            pltpu.VMEM((4, 2, NOV, 9, 2, BLOCK), jnp.bfloat16),
            pltpu.VMEM((4, 2, NOV), jnp.int32),
            pltpu.SMEM((4, 2, NOV), jnp.int32),
            pltpu.SMEM((2,), jnp.int32),
            dma, dma((4,)), dma((4,)), dma((4,)), dma((4,)), dma((4,)), dma((5,)),
            dma((2,)), dma((2,)), dma((8 * CHUNKS,)), dma((8 * CHUNKS,)),
            dma((SLOTS * CHUNKS,)), dma((SLOTS * CHUNKS,)),
        ],
        compiler_params=pltpu.CompilerParams(
            collective_id=0, has_side_effects=True, vmem_limit_bytes=28 * 2**20
        ),
        cost_estimate=pl.CostEstimate(
            flops=2 * 10**9, bytes_accessed=20 * 2**20, transcendentals=0
        ),
    )(*[
        pltpu.with_memory_space_constraint(value, pltpu.HBM)
        for value in (counts, grid, margin, factor, local_inverse)
    ])


def update_kernel(
    counts_ref, sub_ref, live_ref, flipped_ref, local_ref, coupling_ref, diag_ref,
    stage, cross_out, cross_in, c_send, c_recv, k_send, k_recv,
):
    front = lax.axis_index("front")
    row = lax.axis_index("row")
    x, core = front // 2, front % 2
    z, y = row // 4, row % 4
    mine = (y * (1 - core) + z * core) % 2
    count = counts_ref[mine]
    pair_up = partners(x, core, y, z, 1)
    pair_down = partners(x, core, y, z, 3)
    barrier = pltpu.get_barrier_semaphore()
    for other in (pair_up, pair_down):
        pl.semaphore_signal(barrier, inc=1, device_id=other, device_id_type=MESH)

    zero = jnp.zeros((BLOCK, BLOCK), jnp.bfloat16)
    totals = [jnp.zeros((256, 256), jnp.float32) for _ in range(2)]
    sends = []

    def pair(index):
        a = 2 * index
        wide = 8 if index >= 4 else 9
        deep = 8 if index >= 4 else 7

        def block(r, d):
            return sub_ref[r % NOV, d]

        direct = jnp.concatenate(
            [
                jnp.concatenate([block(a, d) for d in range(wide)] + [zero], axis=1),
                jnp.concatenate([zero] + [block(a + 1, d) for d in range(wide)], axis=1),
            ],
            axis=0,
        )
        result = jnp.dot(
            direct, live_ref[a * BLOCK : (a + wide + 1) * BLOCK, :],
            preferred_element_type=jnp.float32,
        )
        mirrored = jnp.concatenate(
            [
                jnp.concatenate([block(a - d, d), block(a - d, d + 1) if d < deep else zero], axis=1)
                if d
                else jnp.concatenate([zero, block(a, 1)], axis=1)
                for d in range(deep, -1, -1)
            ],
            axis=0,
        )
        start = (a + NOV - deep) * BLOCK
        turned = jnp.dot(
            flipped_ref[:, start : start + (deep + 1) * BLOCK], mirrored,
            preferred_element_type=jnp.float32,
        )
        result = -(result + turned.T)
        block_at = a + lax.broadcasted_iota(jnp.int32, result.shape, 0) // BLOCK
        return jnp.where(block_at < count, result, jnp.zeros_like(result)).astype(jnp.bfloat16)

    def send(source, target, send_sem, recv_sem, device):
        copy = pltpu.make_async_remote_copy(
            src_ref=source, dst_ref=target, send_sem=send_sem, recv_sem=recv_sem,
            device_id=device, device_id_type=MESH,
        )
        copy.start()
        sends.append(copy)

    def returned(part, first, number):
        return coupling_ref.at[
            part, pl.ds(first, 512), pl.ds(number * BLOCK, BLOCK)
        ]

    for index in range(8):
        rows = slice(2 * index * BLOCK, (2 * index + 2) * BLOCK)
        result = pair(index)
        coupling_ref[mine, rows, :] = result[:, :256]
        stage[0, rows, :] = result[:, 256:384]
        stage[1, rows, :] = result[:, 384:]
        for number in range(2):
            at = slice(256 * number, 256 * number + 256)
            totals[number] -= jnp.dot(
                flipped_ref[at, rows], result[:, at], preferred_element_type=jnp.float32
            )
        if index == 1:
            pl.semaphore_wait(barrier, 2)
        if index % 2:
            first = (index - 1) * 2 * BLOCK
            for number, device in enumerate((pair_down, pair_up)):
                slot = 2 * (index // 2) + number
                send(
                    stage.at[number, pl.ds(first, 512)], returned(mine, first, number),
                    c_send.at[slot], c_recv.at[slot], device,
                )

    for number, device in enumerate((pair_down, pair_up)):
        at = slice(number * BLOCK, (number + 1) * BLOCK)
        cross_out[number] = totals[1][at, at]
        send(
            cross_out.at[number], cross_in.at[number],
            k_send.at[number], k_recv.at[number], device,
        )
    for number in range(2):
        at = slice(number * BLOCK, (number + 1) * BLOCK)
        diag_ref[mine, number] = local_ref[mine, at, at] + totals[0][at, at]
    for number in range(2):
        at = slice(number * BLOCK, (number + 1) * BLOCK)
        pltpu.make_async_copy(cross_in.at[number], cross_in.at[number], k_recv.at[number]).wait()
        diag_ref[1 - mine, number] = local_ref[1 - mine, at, at] + cross_in[number]
    for quarter in range(4):
        for number in range(2):
            ref = returned(1 - mine, quarter * 512, number)
            pltpu.make_async_copy(ref, ref, c_recv.at[2 * quarter + number]).wait()
    for copy in sends:
        copy.wait_send()


def body(parent, margin, counts, factor, local_inverse):
    sub, live, flipped, local = gathered(parent, margin, counts, factor, local_inverse)
    vmem = pl.BlockSpec(memory_space=pltpu.VMEM)
    dma = pltpu.SemaphoreType.DMA
    return pl.pallas_call(
        update_kernel,
        out_shape=(
            jax.ShapeDtypeStruct(factor.shape, jnp.bfloat16),
            jax.ShapeDtypeStruct((2, 2, BLOCK, BLOCK), jnp.float32),
        ),
        in_specs=[pl.BlockSpec(memory_space=pltpu.SMEM), vmem, vmem, vmem, vmem],
        out_specs=(vmem, vmem),
        scratch_shapes=[
            pltpu.VMEM((2, 2048, BLOCK), jnp.bfloat16),
            pltpu.VMEM((2, BLOCK, BLOCK), jnp.float32),
            pltpu.VMEM((2, BLOCK, BLOCK), jnp.float32),
            dma((8,)), dma((8,)), dma((2,)), dma((2,)),
        ],
        compiler_params=pltpu.CompilerParams(
            collective_id=1, has_side_effects=True, vmem_limit_bytes=24 * 2**20
        ),
        cost_estimate=pl.CostEstimate(
            flops=6 * 10**9, bytes_accessed=20 * 2**20, transcendentals=0
        ),
    )(counts, sub.reshape(NOV, 9, BLOCK, BLOCK), live, flipped, local)


def solution(mesh):
    placed = (
        P(("front", "row"), None),
        P("front", None),
        P("front"),
        P("front", None, "row"),
        P("front", None, "row"),
    )
    return jax.shard_map(
        body,
        mesh=mesh,
        in_specs=placed,
        out_specs=(P("front", None, "row"), P("front", "row", None, None)),
        check_vma=False,
    )
```

time: 95.6 us -> 79.4 us (0.83)
  Pallas kernels: 94.8 us -> 76.6 us
  local copies, waits for them, and re-layouts: 0.01 us -> 2.03 us
    pallas_call x2, Pallas kernels: 94.8 us -> 76.6 us  [the longest x1 63.1 us: gathered(): pl.pallas_call(gather_kernel, out_shape=(jax.ShapeDtypeStruct((NOV, 9, 4,...]
    unnamed x2 -> x4, local copies, waits for them, and re-layouts: 0.01 us -> 2.03 us
where the time goes in v4:
time: 79.4 us; the launch traced here: 79.2 us
  Pallas kernels  76.6 us (96%)
  local copies, waits for them, and re-layouts  2.03 us (3%)
    pallas_call x1, Pallas kernels, gathered(): pl.pallas_call(gather_kernel, out_shape=(jax.ShapeDtypeStruct((NOV, 9, 4,...  63.1 us
    pallas_call x1, Pallas kernels, body(): pl.pallas_call(update_kernel, out_shape=(jax.ShapeDtypeStruct(factor.shap...  13.4 us
    unnamed x4, local copies, waits for them, and re-layouts  2.03 us

profile of v4, /device:TPU:0, one launch (start us, length us, event | category | flops | bytes accessed | tf_op | source)
XLA Modules:
  0.0 79.2 jit_solution(12337221968679486517)
XLA Ops:
  0.6 0.0 copy-start
  0.6 63.1 %shard_map.68 = (bf16[16,9,4,4,4,2,128]{6,5,4,3,2,1,0:T(2,128)(2,1)S(1)}, bf16[4096,512]{1,0:T(8,128)(2,1)S(1)}, bf16[512,4096]{1,0:T(8,128)(2,1)S(1)}, f32[2,256,256]{2,1,0:T(8,128)S(1)}) custom-call(s32[2]{0:T(128)} %counts_ref.3, bf16[8,64,4,2,128]{4,3,2,1,0:T(2,128)(2,1)} %bitcast.5, s32[2,16]{1,0:T(2,128)} %margin_ref.1, ...), custom_call_target="tpu_custom_call" | custom-call | flops 2000000000 | bytes 20971520 | tf_op jit(solution)/shard_map/pallas_call | solution.py:330
  63.8 0.0 copy-done
  63.8 13.4 %shard_map.69 = (bf16[2,2048,256]{2,1,0:T(8,128)(2,1)S(1)}, f32[2,2,128,128]{3,2,1,0:T(8,128)S(1)}) custom-call(s32[2]{0:T(128)S(1)} %copy-done, bf16[16,9,128,128]{3,2,1,0:T(8,128)(2,1)S(1)} %bitcast.4, bf16[4096,512]{1,0:T(8,128)(2,1)S(1)} %get-tuple-element.7.live_ref, bf16[512,4096]{1,0:T(8,128)(2,1)S(1)} %get-tuple-element.8.flipped_ref, ...), custom_call_target="tpu_custom_call" | custom-call | flops 6000000000 | bytes 20971520 | tf_op jit(solution)/shard_map/pallas_call | solution.py:485
  77.2 1.3 %copy.9 = bf16[2,2048,256]{2,1,0:T(8,128)(2,1)} copy(bf16[2,2048,256]{2,1,0:T(8,128)(2,1)S(1)} %get-tuple-element.12) | data formatting | bytes 4194304
  78.5 0.7 copy.10
Async XLA Ops:
  0.6 63.2 %copy-start = (s32[2]{0:T(128)S(1)}, s32[2]{0:T(128)}, u32[]{:S(2)}) copy-start(s32[2]{0:T(128)} %counts_ref.3) | copy-start | bytes 28

commit v5 on v4

v5 whole, which is shorter than its diff:
```python
import functools

import jax
import jax.numpy as jnp
from jax import lax
from jax.experimental import pallas as pl
from jax.experimental.pallas import tpu as pltpu
from jax.sharding import PartitionSpec as P

MESH = pl.DeviceIdType.MESH
NOV = 16
BLOCK = 128
BLOCKS = 136
CUTS = (0, 5, 16)
CHUNKS = len(CUTS) - 1
SLOTS = 20


def place(x, core, y, z):
    return (2 * x + core, 4 * z + y)


def first_block(a):
    return NOV * a - a * (a - 1) // 2


def order(block):
    x, core, z, yh = block >> 4, (block >> 3) & 1, (block >> 1) & 3, block & 1
    group = z * (1 - core) + (7 - z) * core
    return group * 8 + x * 2 + yh


def network(count):
    swaps, p = [], 1
    while p < count:
        k = p
        while k >= 1:
            for j in range(k % p, count - k, 2 * k):
                for i in range(min(k, count - j - k)):
                    if (i + j) // (2 * p) == (i + j + k) // (2 * p):
                        swaps.append((i + j, i + j + k))
            k //= 2
        p *= 2
    return swaps


def columns(core, z):
    return (2 * z, 16 - 2 * z) if core == 0 else (8, 2 * z + 2)


def spans(chunk):
    first, last = first_block(CUTS[chunk]), first_block(CUTS[chunk + 1])
    return first, last - first


def partners(x, core, y, z, up):
    return place(x, core, (y + up * (1 - core)) % 4, (z + up * core) % 4)


def others(x, core, y, z, up):
    return place(x, core, (y + up * core) % 4, (z + up * (1 - core)) % 4)


def prepare_factor(
    count, part, ranked, factor_buf, lent_buf, live_ref, flipped_ref, alive_ref
):
    def mask(at, _):
        a = ranked(at)
        rows = pl.multiple_of(at * BLOCK, BLOCK)
        value = jnp.concatenate([factor_buf[part, a], lent_buf[0, a], lent_buf[1, a]], axis=1)
        value = jnp.where(a < count, value, jnp.zeros_like(value))
        live_ref[pl.ds(rows, BLOCK), :] = value
        flipped_ref[:, pl.ds(rows, BLOCK)] = value.T
        ones = jnp.ones((8, 512), jnp.float32)
        alive_ref[at] = jnp.where(a < count, ones, jnp.zeros_like(ones))
        return 0

    lax.fori_loop(0, NOV, mask, 0)


def prepare_local(part, first_col, inverse_buf, local_ref):
    def local(step, total):
        rows = pl.multiple_of(step * 512, 512)
        value = inverse_buf[part, pl.ds(rows, 512), :]
        row_at = rows + lax.broadcasted_iota(jnp.int32, value.shape, 0)
        col_at = first_col + lax.broadcasted_iota(jnp.int32, value.shape, 1)
        value = jnp.where(row_at >= col_at, value, jnp.zeros_like(value))
        return total + lax.dot_general(
            value, value, (((0,), (0,)), ((), ())), preferred_element_type=jnp.float32
        )

    local_ref[part] = lax.fori_loop(0, 8, local, jnp.zeros((256, 256), jnp.float32))


def gather_kernel(
    counts_ref, parent_ref, margin_ref, factor_ref, inverse_ref,
    out_ref, live_ref, flipped_ref, alive_ref, local_ref,
    parent_buf, factor_buf, inverse_buf, lent_buf, other_buf, slabs, picked, margin_buf, margin_smem, sorted_smem, ranked_smem, counts_smem,
    t_send, t_recv, d_send, d_recv, m_send, m_recv, l_sem, f_send, f_recv, x_send, x_recv, g_send, g_recv,
):
    front = lax.axis_index("front")
    row = lax.axis_index("row")
    x, core = front // 2, front % 2
    z, y = row // 4, row % 4
    half, yh = y % 2, y // 2
    fold = half * 2 + yh
    me_q = yh * 16 + z * 4 + x
    my_block = 16 * x + 8 * core + 2 * z + yh
    here = y * (1 - core) + z * core
    there = z * (1 - core) + y * core
    mine = here % 2
    sibling = place(x, 1 - core, y, z)
    pair_up = partners(x, core, y, z, 1)
    pair_down = partners(x, core, y, z, 3)
    pair_far = partners(x, core, y, z, 2)
    ring_up = others(x, core, y, z, 1)
    ring_down = others(x, core, y, z, 3)
    y_up = place(x, core, (y + 1) % 4, z)
    y_down = place(x, core, (y + 3) % 4, z)

    def member(q):
        return place(q % 4, core, 2 * (q // 16) + half, (q // 4) % 4)

    parent_load = pltpu.make_async_copy(parent_ref, parent_buf, l_sem.at[0])
    parent_load.start()
    factor_load = pltpu.make_async_copy(factor_ref, factor_buf, l_sem.at[1])
    factor_load.start()
    inverse_load = pltpu.make_async_copy(inverse_ref, inverse_buf, l_sem.at[2])
    inverse_load.start()
    counts_load = pltpu.make_async_copy(counts_ref, counts_smem, l_sem.at[4])
    counts_load.start()

    barrier = pltpu.get_barrier_semaphore()

    def greet(step, _):
        pl.semaphore_signal(
            barrier, inc=1, device_id=member((me_q + step) % 32), device_id_type=MESH
        )
        return 0

    lax.fori_loop(1, 32, greet, 0)
    for other in (sibling, y_up, y_down):
        pl.semaphore_signal(barrier, inc=1, device_id=other, device_id_type=MESH)
    parent_load.wait()
    pl.semaphore_wait(barrier, 34)

    margin_sends = []
    for step in (1, 2, 3):
        copy = pltpu.make_async_remote_copy(
            src_ref=margin_ref,
            dst_ref=margin_buf.at[x],
            send_sem=m_send.at[step],
            recv_sem=m_recv.at[x],
            device_id=place((x + step) % 4, core, y, z),
            device_id_type=MESH,
        )
        copy.start()
        margin_sends.append(copy)
    pltpu.make_async_copy(margin_ref, margin_buf.at[x], m_recv.at[x]).start()

    def spread_all(own_core, own_z):
        cols = pl.ds(*columns(own_core, own_z))
        pltpu.make_async_copy(
            parent_buf.at[me_q // 4, :, cols, me_q % 4],
            slabs.at[my_block, :, cols],
            t_recv.at[x],
        ).start()
        for offset in (0, 1, 3, 2):

            def spread(step, _):
                q = (yh * 4 + z + step) % 8 * 4 + (x + offset) % 4
                pltpu.make_async_remote_copy(
                    src_ref=parent_buf.at[q // 4, :, cols, q % 4],
                    dst_ref=slabs.at[my_block, :, cols],
                    send_sem=t_send,
                    recv_sem=t_recv.at[x],
                    device_id=member(q),
                    device_id_type=MESH,
                ).start()
                return 0

            lax.fori_loop(0 if offset else 1, 8, spread, 0)

    for own_core in range(2):
        for own_z in range(4):
            pl.when(jnp.logical_and(core == own_core, z == own_z))(
                functools.partial(spread_all, own_core, own_z)
            )

    for source in range(4):
        pltpu.make_async_copy(margin_ref, margin_buf.at[source], m_recv.at[source]).wait()
    to_smem = pltpu.make_async_copy(margin_buf, margin_smem, l_sem.at[3])
    to_smem.start()
    to_smem.wait()

    swaps = network(NOV)

    def sort(index, _):
        target, part = index // 2, index % 2
        keys = []
        for a in range(NOV):
            block = margin_smem[target, part, a]
            keys.append(order(block) * 1024 + block * NOV + a)
        for i, j in swaps:
            keys[i], keys[j] = jnp.minimum(keys[i], keys[j]), jnp.maximum(keys[i], keys[j])
        for a in range(NOV):
            sorted_smem[target, part, a] = (keys[a] >> 4) & 63
            ranked_smem[target, part, a] = keys[a] & (NOV - 1)
        return 0

    lax.fori_loop(0, 8, sort, 0)

    def swap_cores(own_core, wait_only):
        total = sum(columns(own_core, own_z)[1] for own_z in range(4)) // 4
        for offset in (0, 1, 3, 2):
            source = (x + 4 - offset) % 4
            if not wait_only:
                group = slabs.at[pl.ds(0, 8), :, pl.ds(0, total)]
                pltpu.make_async_copy(group, group, t_recv.at[source]).wait()
            for own_z in range(4):
                part = slabs.at[
                    pl.ds(16 * source + 8 * own_core + 2 * own_z, 2), :,
                    pl.ds(*columns(own_core, own_z)),
                ]
                slot = 4 * source + own_z
                if wait_only:
                    pltpu.make_async_copy(part, part, d_recv.at[slot]).wait()
                else:
                    pltpu.make_async_remote_copy(
                        src_ref=part,
                        dst_ref=part,
                        send_sem=d_send.at[slot],
                        recv_sem=d_recv.at[slot],
                        device_id=sibling,
                        device_id_type=MESH,
                    ).start()

    def swap_sent(own_core):
        for source in range(4):
            for own_z in range(4):
                part = slabs.at[
                    pl.ds(16 * source + 8 * own_core + 2 * own_z, 2), :,
                    pl.ds(*columns(own_core, own_z)),
                ]
                pltpu.make_async_copy(part, part, d_send.at[4 * source + own_z]).wait()

    for own_core in range(2):
        pl.when(core == own_core)(functools.partial(swap_cores, own_core, False))

    factor_load.wait()
    lends = []
    for number, device in enumerate((pair_up, pair_down)):
        copy = pltpu.make_async_remote_copy(
            src_ref=factor_buf.at[1 - mine, :, :, pl.ds(number * BLOCK, BLOCK)],
            dst_ref=lent_buf.at[number],
            send_sem=f_send.at[number],
            recv_sem=f_recv.at[number],
            device_id=device,
            device_id_type=MESH,
        )
        copy.start()
        lends.append(copy)

    for own_core in range(2):
        pl.when(core == 1 - own_core)(functools.partial(swap_cores, own_core, True))

    x_copies = [[] for _ in range(CHUNKS)]

    def start_x(chunk):
        blocks = pl.ds(*spans(chunk))
        for step in (2, 1, 3, 0):
            target = (x + step) % 4

            def pick(part, _):
                ids = [sorted_smem[target, part, a] for a in range(NOV)]
                for a in range(CUTS[chunk], CUTS[chunk + 1]):
                    for b in range(a, NOV):
                        block = slabs[ids[a], ids[b] >> 4, ids[b] & 15]
                        picked[target, part, first_block(a) + b - a] = block
                return 0

            lax.fori_loop(0, 2, pick, 0)
            slot = 8 * chunk + 2 * step
            lands = (out_ref.at[blocks, fold, z, x], other_buf.at[blocks, x])
            for number, land in enumerate(lands):
                part = (mine + number) % 2
                if step:
                    copy = pltpu.make_async_remote_copy(
                        src_ref=picked.at[target, part, blocks],
                        dst_ref=land,
                        send_sem=x_send.at[slot + number],
                        recv_sem=x_recv.at[slot + number],
                        device_id=place(target, core, y, z),
                        device_id_type=MESH,
                    )
                else:
                    copy = pltpu.make_async_copy(
                        picked.at[target, part, blocks], land, x_recv.at[slot + number]
                    )
                copy.start()
                x_copies[chunk].append(copy)

    sends = []

    def piece(chunk, pair_at, ring_at, side=None):
        y_at = pair_at * (1 - core) + ring_at * core
        z_at = ring_at * (1 - core) + pair_at * core
        first, count = spans(chunk)
        if side == 0:
            count = count // 2
        if side == 1:
            first, count = first + count // 2, count - count // 2
        return out_ref.at[pl.ds(first, count), (y_at % 2) * 2 + y_at // 2, z_at]

    def send(chunk, slot, source, target, device):
        at = SLOTS * chunk + slot
        copy = pltpu.make_async_remote_copy(
            src_ref=source, dst_ref=target, send_sem=g_send.at[at], recv_sem=g_recv.at[at],
            device_id=device, device_id_type=MESH,
        )
        copy.start()
        sends.append(copy)

    def landed(chunk, slot, ref):
        pltpu.make_async_copy(ref, ref, g_recv.at[SLOTS * chunk + slot]).wait()

    pair_places = (here, (here + 3) % 4, (here + 1) % 4, (here + 2) % 4)
    above, below, far = (there + 1) % 4, (there + 3) % 4, (there + 2) % 4

    def ring_direct(chunk, number):
        own = piece(chunk, pair_places[number], there)
        send(chunk, 4 + 4 * number, own, own, ring_up)
        send(chunk, 5 + 4 * number, own, own, ring_down)

    def ring_forward(chunk, number):
        at = pair_places[number]
        landed(chunk, 4 + 4 * number, piece(chunk, at, below))
        low = piece(chunk, at, below, 0)
        send(chunk, 6 + 4 * number, low, low, ring_up)
        landed(chunk, 5 + 4 * number, piece(chunk, at, above))
        high = piece(chunk, at, above, 1)
        send(chunk, 7 + 4 * number, high, high, ring_down)

    def step_own(chunk):
        for copy in x_copies[chunk]:
            copy.wait()
        own = piece(chunk, here, there)
        other = other_buf.at[pl.ds(*spans(chunk))]
        send(chunk, 0, other, own, pair_up)
        send(chunk, 1, other, own, pair_down)
        send(chunk, 2, own, own, pair_far)
        ring_direct(chunk, 0)

    def step_near(chunk):
        for number in (1, 2, 3):
            landed(chunk, number - 1, piece(chunk, pair_places[number], there))
            ring_direct(chunk, number)
        ring_forward(chunk, 0)

    def step_far(chunk):
        for number in (1, 2, 3):
            ring_forward(chunk, number)

    def step_end(chunk):
        for number, at in enumerate(pair_places):
            landed(chunk, 6 + 4 * number, piece(chunk, at, far, 0))
            landed(chunk, 7 + 4 * number, piece(chunk, at, far, 1))

    start_x(0)
    start_x(1)
    for turn in range(CHUNKS + 3):
        for delay, step in enumerate((step_own, step_near, step_far, step_end)):
            if 0 <= turn - delay < CHUNKS:
                step(turn - delay)
                if delay == 0 and turn + 2 < CHUNKS:
                    start_x(turn + 2)
        if turn == min(1, CHUNKS - 1):
            for copy in lends:
                copy.wait()
            counts_load.wait()
            prepare_factor(
                counts_smem[mine], mine, lambda at: ranked_smem[x, mine, at],
                factor_buf, lent_buf, live_ref, flipped_ref, alive_ref,
            )
        if turn == min(2, CHUNKS):
            inverse_load.wait()
            for part in range(2):
                prepare_local(part, row * 256, inverse_buf, local_ref)

    for copy in sends:
        copy.wait_send()
    for copy in margin_sends:
        copy.wait_send()

    def spread_sent(own_core, own_z):
        sent = slabs.at[pl.ds(0, 31), :, pl.ds(0, columns(own_core, own_z)[1])]
        pltpu.make_async_copy(sent, sent, t_send).wait()

    for own_core in range(2):
        pl.when(core == own_core)(functools.partial(swap_sent, own_core))
        for own_z in range(4):
            pl.when(jnp.logical_and(core == own_core, z == own_z))(
                functools.partial(spread_sent, own_core, own_z)
            )


def gathered(parent, margin, counts, factor, local_inverse):
    grid = parent.reshape(8, 4, 2, 4, 16, BLOCK).transpose(0, 3, 4, 1, 2, 5)
    factor = factor.reshape(2, NOV, BLOCK, 256)
    dma = pltpu.SemaphoreType.DMA
    vmem = pl.BlockSpec(memory_space=pltpu.VMEM)
    hbm = pl.BlockSpec(memory_space=pltpu.HBM)
    return pl.pallas_call(
        gather_kernel,
        out_shape=(
            jax.ShapeDtypeStruct((BLOCKS, 4, 4, 4, 2, BLOCK), jnp.bfloat16),
            jax.ShapeDtypeStruct((2048, 512), jnp.bfloat16),
            jax.ShapeDtypeStruct((512, 2048), jnp.bfloat16),
            jax.ShapeDtypeStruct((NOV, 8, 512), jnp.float32),
            jax.ShapeDtypeStruct((2, 256, 256), jnp.float32),
        ),
        in_specs=[hbm] * 5,
        out_specs=(vmem,) * 5,
        scratch_shapes=[
            pltpu.VMEM(grid.shape, jnp.bfloat16),
            pltpu.VMEM(factor.shape, jnp.bfloat16),
            pltpu.VMEM(local_inverse.shape, jnp.bfloat16),
            pltpu.VMEM((2, NOV, BLOCK, BLOCK), jnp.bfloat16),
            pltpu.VMEM((BLOCKS, 4, 2, BLOCK), jnp.bfloat16),
            pltpu.VMEM((64, 4, 16, 2, BLOCK), jnp.bfloat16),
            pltpu.VMEM((4, 2, BLOCKS, 2, BLOCK), jnp.bfloat16),
            pltpu.VMEM((4, 2, NOV), jnp.int32),
            pltpu.SMEM((4, 2, NOV), jnp.int32),
            pltpu.SMEM((4, 2, NOV), jnp.int32),
            pltpu.SMEM((4, 2, NOV), jnp.int32),
            pltpu.SMEM((2,), jnp.int32),
            dma, dma((4,)), dma((16,)), dma((16,)), dma((4,)), dma((4,)), dma((5,)),
            dma((2,)), dma((2,)), dma((8 * CHUNKS,)), dma((8 * CHUNKS,)),
            dma((SLOTS * CHUNKS,)), dma((SLOTS * CHUNKS,)),
        ],
        compiler_params=pltpu.CompilerParams(
            collective_id=0, has_side_effects=True, vmem_limit_bytes=28 * 2**20
        ),
        cost_estimate=pl.CostEstimate(
            flops=2 * 10**9, bytes_accessed=20 * 2**20, transcendentals=0
        ),
    )(*[
        pltpu.with_memory_space_constraint(value, pltpu.HBM)
        for value in (counts, grid, margin, factor, local_inverse)
    ])


def update_kernel(
    margin_ref, sub_ref, live_ref, flipped_ref, alive_ref, local_ref, coupling_ref, diag_ref,
    ordered, rank_smem, stage, cross_out, cross_in, c_send, c_recv, k_send, k_recv,
):
    front = lax.axis_index("front")
    row = lax.axis_index("row")
    x, core = front // 2, front % 2
    z, y = row // 4, row % 4
    mine = (y * (1 - core) + z * core) % 2
    pair_up = partners(x, core, y, z, 1)
    pair_down = partners(x, core, y, z, 3)
    barrier = pltpu.get_barrier_semaphore()
    for other in (pair_up, pair_down):
        pl.semaphore_signal(barrier, inc=1, device_id=other, device_id_type=MESH)

    def rank(part, _):
        keys = [order(margin_ref[part, a]) for a in range(NOV)]
        for a in range(NOV):
            rank_smem[part, a] = sum((keys[b] < keys[a]).astype(jnp.int32) for b in range(NOV) if b != a)
        return 0


    totals = [jnp.zeros((256, 256), jnp.float32) for _ in range(2)]
    sends = []

    def block(a, b):
        return sub_ref[first_block(a) + b - a]

    def pair(index):
        a = 2 * index
        direct = jnp.concatenate(
            [
                jnp.concatenate([block(a, b) for b in range(a, NOV)], axis=1),
                jnp.concatenate(
                    [block(a, a + 1).T] + [block(a + 1, b) for b in range(a + 1, NOV)], axis=1
                ),
            ],
            axis=0,
        )
        result = jnp.dot(direct, live_ref[a * BLOCK :, :], preferred_element_type=jnp.float32)
        if index:
            mirrored = jnp.concatenate(
                [jnp.concatenate([block(b, a), block(b, a + 1)], axis=1) for b in range(a)], axis=0
            )
            turned = jnp.dot(
                flipped_ref[:, : a * BLOCK], mirrored, preferred_element_type=jnp.float32
            )
            result = result + turned.T
        halves = []
        for half in range(2):
            value = -result[half * BLOCK : (half + 1) * BLOCK]
            value = jnp.where(alive_ref[a + half, :1, :] > 0, value, jnp.zeros_like(value))
            halves.append(value.astype(jnp.bfloat16))
        return halves

    def send(source, target, send_sem, recv_sem, device):
        copy = pltpu.make_async_remote_copy(
            src_ref=source, dst_ref=target, send_sem=send_sem, recv_sem=recv_sem,
            device_id=device, device_id_type=MESH,
        )
        copy.start()
        sends.append(copy)

    def returned(part, first, number):
        return ordered.at[part, pl.ds(first, 4), :, pl.ds(number * BLOCK, BLOCK)]

    for index in range(8):
        rows = slice(2 * index * BLOCK, (2 * index + 2) * BLOCK)
        halves = pair(index)
        for half in range(2):
            ordered[mine, 2 * index + half] = halves[half][:, :256]
            stage[0, 2 * index + half] = halves[half][:, 256:384]
            stage[1, 2 * index + half] = halves[half][:, 384:]
        result = jnp.concatenate(halves, axis=0)
        for number in range(2):
            at = slice(256 * number, 256 * number + 256)
            totals[number] -= jnp.dot(
                flipped_ref[at, rows], result[:, at], preferred_element_type=jnp.float32
            )
        if index == 1:
            pl.semaphore_wait(barrier, 2)
        if index % 2:
            first = 2 * index - 2
            for number, device in enumerate((pair_down, pair_up)):
                slot = 2 * (index // 2) + number
                send(
                    stage.at[number, pl.ds(first, 4)], returned(mine, first, number),
                    c_send.at[slot], c_recv.at[slot], device,
                )

    for number, device in enumerate((pair_down, pair_up)):
        at = slice(number * BLOCK, (number + 1) * BLOCK)
        cross_out[number] = totals[1][at, at]
        send(
            cross_out.at[number], cross_in.at[number],
            k_send.at[number], k_recv.at[number], device,
        )
    for number in range(2):
        at = slice(number * BLOCK, (number + 1) * BLOCK)
        diag_ref[mine, number] = local_ref[mine, at, at] + totals[0][at, at]
    def restore(part):
        def one(a, _):
            rows = pl.multiple_of(a * BLOCK, BLOCK)
            coupling_ref[part, pl.ds(rows, BLOCK), :] = ordered[part, rank_smem[part, a]]
            return 0

        lax.fori_loop(0, NOV, one, 0)

    for number in range(2):
        at = slice(number * BLOCK, (number + 1) * BLOCK)
        pltpu.make_async_copy(cross_in.at[number], cross_in.at[number], k_recv.at[number]).wait()
        diag_ref[1 - mine, number] = local_ref[1 - mine, at, at] + cross_in[number]
    lax.fori_loop(0, 2, rank, 0)
    for quarter in range(4):
        for number in range(2):
            ref = returned(1 - mine, quarter * 4, number)
            pltpu.make_async_copy(ref, ref, c_recv.at[2 * quarter + number]).wait()
    restore(mine)
    restore(1 - mine)
    for copy in sends:
        copy.wait_send()


def body(parent, margin, counts, factor, local_inverse):
    sub, live, flipped, alive, local = gathered(parent, margin, counts, factor, local_inverse)
    vmem = pl.BlockSpec(memory_space=pltpu.VMEM)
    dma = pltpu.SemaphoreType.DMA
    return pl.pallas_call(
        update_kernel,
        out_shape=(
            jax.ShapeDtypeStruct(factor.shape, jnp.bfloat16),
            jax.ShapeDtypeStruct((2, 2, BLOCK, BLOCK), jnp.float32),
        ),
        in_specs=[pl.BlockSpec(memory_space=pltpu.SMEM)] + [vmem] * 5,
        out_specs=(vmem, vmem),
        scratch_shapes=[
            pltpu.VMEM((2, NOV, BLOCK, 256), jnp.bfloat16),
            pltpu.SMEM((2, NOV), jnp.int32),
            pltpu.VMEM((2, NOV, BLOCK, BLOCK), jnp.bfloat16),
            pltpu.VMEM((2, BLOCK, BLOCK), jnp.float32),
            pltpu.VMEM((2, BLOCK, BLOCK), jnp.float32),
            dma((8,)), dma((8,)), dma((2,)), dma((2,)),
        ],
        compiler_params=pltpu.CompilerParams(
            collective_id=1, has_side_effects=True, vmem_limit_bytes=24 * 2**20
        ),
        cost_estimate=pl.CostEstimate(
            flops=6 * 10**9, bytes_accessed=20 * 2**20, transcendentals=0
        ),
    )(margin, sub.reshape(BLOCKS, BLOCK, BLOCK), live, flipped, alive, local)


def solution(mesh):
    placed = (
        P(("front", "row"), None),
        P("front", None),
        P("front"),
        P("front", None, "row"),
        P("front", None, "row"),
    )
    return jax.shard_map(
        body,
        mesh=mesh,
        in_specs=placed,
        out_specs=(P("front", None, "row"), P("front", "row", None, None)),
        check_vma=False,
    )
```

time: 79.4 us -> 73.6 us (0.927)
  Pallas kernels: 76.6 us -> 70.7 us
    pallas_call x1, Pallas kernels: 63.1 us -> 55.4 us  [gathered(): pl.pallas_call(gather_kernel, out_shape=(jax.ShapeDtypeStruct((BLOCKS, 4,...]
    pallas_call x1, Pallas kernels: 13.4 us -> 15.2 us  [body(): pl.pallas_call(update_kernel, out_shape=(jax.ShapeDtypeStruct(factor.shap...]
where the time goes in v5:
time: 73.6 us; the launch traced here: 73.4 us
  Pallas kernels  70.7 us (96%)
  local copies, waits for them, and re-layouts  2.03 us (3%)
    pallas_call x1, Pallas kernels, gathered(): pl.pallas_call(gather_kernel, out_shape=(jax.ShapeDtypeStruct((BLOCKS, 4,...  55.4 us
    pallas_call x1, Pallas kernels, body(): pl.pallas_call(update_kernel, out_shape=(jax.ShapeDtypeStruct(factor.shap...  15.2 us
    unnamed x4, local copies, waits for them, and re-layouts  2.03 us

profile of v5, /device:TPU:0, one launch (start us, length us, event | category | flops | bytes accessed | tf_op | source)
XLA Modules:
  0.0 73.4 jit_solution(4621560160783650237)
XLA Ops:
  0.6 0.0 copy-start
  0.6 55.4 %shard_map.68 = (bf16[136,4,4,4,2,128]{5,4,3,2,1,0:T(2,128)(2,1)S(1)}, bf16[2048,512]{1,0:T(8,128)(2,1)S(1)}, bf16[512,2048]{1,0:T(8,128)(2,1)S(1)}, f32[16,8,512]{2,1,0:T(8,128)S(1)}, f32[2,256,256]{2,1,0:T(8,128)S(1)}) custom-call(s32[2]{0:T(128)} %counts_ref.1, bf16[8,4,16,4,2,128]{5,4,3,2,1,0:T(2,128)(2,1)} %bitcast.7, s32[2,16]{1,0:T(2,128)} %margin_ref.3, ...), custom_call_target="tpu_custom_call" | custom-call | flops 2000000000 | bytes 20971520 | tf_op jit(solution)/shard_map/pallas_call | solution.py:413
  56.1 0.0 copy-done
  56.1 15.2 %shard_map.69 = (bf16[2,2048,256]{2,1,0:T(8,128)(2,1)S(1)}, f32[2,2,128,128]{3,2,1,0:T(8,128)S(1)}) custom-call(s32[2,16]{1,0:T(2,128)S(1)} %copy-done, bf16[136,128,128]{2,1,0:T(8,128)(2,1)S(1)} %bitcast.5, bf16[2048,512]{1,0:T(8,128)(2,1)S(1)} %get-tuple-element.8.live_ref, bf16[512,2048]{1,0:T(8,128)(2,1)S(1)} %get-tuple-element.9.flipped_ref, ...), custom_call_target="tpu_custom_call" | custom-call | flops 6000000000 | bytes 20971520 | tf_op jit(solution)/shard_map/pallas_call | solution.py:580
  71.4 1.3 %copy.9 = bf16[2,2048,256]{2,1,0:T(8,128)(2,1)} copy(bf16[2,2048,256]{2,1,0:T(8,128)(2,1)S(1)} %get-tuple-element.14) | data formatting | bytes 4194304
  72.7 0.7 copy.10
Async XLA Ops:
  0.6 55.5 %copy-start = (s32[2,16]{1,0:T(2,128)S(1)}, s32[2,16]{1,0:T(2,128)}, u32[]{:S(2)}) copy-start(s32[2,16]{1,0:T(2,128)} %margin_ref.3) | copy-start | bytes 388

commit v6 on v5

--- a/solution.py
+++ b/solution.py
@@ -11,7 +11,7 @@
 NOV = 16
 BLOCK = 128
 BLOCKS = 136
-CUTS = (0, 5, 16)
+CUTS = (0, 3, 16)
 CHUNKS = len(CUTS) - 1
 SLOTS = 20
 
@@ -472,13 +472,12 @@
         return 0
 
 
-    totals = [jnp.zeros((256, 256), jnp.float32) for _ in range(2)]
     sends = []
 
     def block(a, b):
         return sub_ref[first_block(a) + b - a]
 
-    def pair(index):
+    def pair(index, cols):
         a = 2 * index
         direct = jnp.concatenate(
             [
@@ -489,19 +488,19 @@
             ],
             axis=0,
         )
-        result = jnp.dot(direct, live_ref[a * BLOCK :, :], preferred_element_type=jnp.float32)
+        result = jnp.dot(direct, live_ref[a * BLOCK :, cols], preferred_element_type=jnp.float32)
         if index:
             mirrored = jnp.concatenate(
                 [jnp.concatenate([block(b, a), block(b, a + 1)], axis=1) for b in range(a)], axis=0
             )
             turned = jnp.dot(
-                flipped_ref[:, : a * BLOCK], mirrored, preferred_element_type=jnp.float32
+                flipped_ref[cols, : a * BLOCK], mirrored, preferred_element_type=jnp.float32
             )
             result = result + turned.T
         halves = []
         for half in range(2):
             value = -result[half * BLOCK : (half + 1) * BLOCK]
-            value = jnp.where(alive_ref[a + half, :1, :] > 0, value, jnp.zeros_like(value))
+            value = jnp.where(alive_ref[a + half, :1, : cols.stop - cols.start] > 0, value, jnp.zeros_like(value))
             halves.append(value.astype(jnp.bfloat16))
         return halves
 
@@ -516,53 +515,66 @@
     def returned(part, first, number):
         return ordered.at[part, pl.ds(first, 4), :, pl.ds(number * BLOCK, BLOCK)]
 
-    for index in range(8):
-        rows = slice(2 * index * BLOCK, (2 * index + 2) * BLOCK)
-        halves = pair(index)
+    def cross(cols, value):
+        return jnp.dot(
+            flipped_ref[cols, :], value.reshape(NOV * BLOCK, 256),
+            preferred_element_type=jnp.float32,
+        )
+
+    own, lent, both = slice(0, 256), slice(256, 512), slice(0, 512)
+    for part in range(2):
+        rank(part, 0)
+    order_of_work = [(index, both) for index in range(4)]
+    order_of_work += [(index, lent) for index in range(4, 8)]
+    order_of_work += [(index, own) for index in range(4, 8)]
+    for index, cols in order_of_work:
+        halves = pair(index, cols)
         for half in range(2):
-            ordered[mine, 2 * index + half] = halves[half][:, :256]
-            stage[0, 2 * index + half] = halves[half][:, 256:384]
-            stage[1, 2 * index + half] = halves[half][:, 384:]
-        result = jnp.concatenate(halves, axis=0)
-        for number in range(2):
-            at = slice(256 * number, 256 * number + 256)
-            totals[number] -= jnp.dot(
-                flipped_ref[at, rows], result[:, at], preferred_element_type=jnp.float32
-            )
+            at = 2 * index + half
+            if cols is not lent:
+                ordered[mine, at] = halves[half][:, :256]
+            if cols is not own:
+                stage[0, at] = halves[half][:, -256:-128]
+                stage[1, at] = halves[half][:, -128:]
+        if cols is own:
+            continue
         if index == 1:
             pl.semaphore_wait(barrier, 2)
-        if index % 2:
-            first = 2 * index - 2
+        if index % 2 == 2 - 1 and index:
+            for done in (0, 1) if index == 1 and 2 == 1 else (index // 2,):
+                for number, device in enumerate((pair_down, pair_up)):
+                    slot = 2 * done + number
+                    send(
+                        stage.at[number, pl.ds(4 * done, 4)],
+                        returned(mine, 4 * done, number),
+                        c_send.at[slot], c_recv.at[slot], device,
+                    )
+        if index == 7:
+            total = cross(lent, jnp.concatenate([stage[0], stage[1]], axis=2))
             for number, device in enumerate((pair_down, pair_up)):
-                slot = 2 * (index // 2) + number
+                at = slice(number * BLOCK, (number + 1) * BLOCK)
+                cross_out[number] = -total[at, at]
                 send(
-                    stage.at[number, pl.ds(first, 4)], returned(mine, first, number),
-                    c_send.at[slot], c_recv.at[slot], device,
+                    cross_out.at[number], cross_in.at[number],
+                    k_send.at[number], k_recv.at[number], device,
                 )
-
-    for number, device in enumerate((pair_down, pair_up)):
-        at = slice(number * BLOCK, (number + 1) * BLOCK)
-        cross_out[number] = totals[1][at, at]
-        send(
-            cross_out.at[number], cross_in.at[number],
-            k_send.at[number], k_recv.at[number], device,
-        )
+    total = cross(own, ordered[mine])
+
     for number in range(2):
         at = slice(number * BLOCK, (number + 1) * BLOCK)
-        diag_ref[mine, number] = local_ref[mine, at, at] + totals[0][at, at]
+        diag_ref[mine, number] = local_ref[mine, at, at] - total[at, at]
     def restore(part):
         def one(a, _):
             rows = pl.multiple_of(a * BLOCK, BLOCK)
             coupling_ref[part, pl.ds(rows, BLOCK), :] = ordered[part, rank_smem[part, a]]
             return 0
 
-        lax.fori_loop(0, NOV, one, 0)
+        lax.fori_loop(0, NOV, one, 0, unroll=4)
 
     for number in range(2):
         at = slice(number * BLOCK, (number + 1) * BLOCK)
         pltpu.make_async_copy(cross_in.at[number], cross_in.at[number], k_recv.at[number]).wait()
         diag_ref[1 - mine, number] = local_ref[1 - mine, at, at] + cross_in[number]
-    lax.fori_loop(0, 2, rank, 0)
     for quarter in range(4):
         for number in range(2):
             ref = returned(1 - mine, quarter * 4, number)

time: 73.6 us -> 70.5 us (0.958)
  Pallas kernels: 70.7 us -> 67.5 us
    pallas_call x1, Pallas kernels: 15.2 us -> 12.7 us  [body(): pl.pallas_call(update_kernel, out_shape=(jax.ShapeDtypeStruct(factor.shap...]
where the time goes in v6:
time: 70.5 us; the launch traced here: 70.2 us
  Pallas kernels  67.5 us (96%)
  local copies, waits for them, and re-layouts  2.03 us (3%)
    pallas_call x1, Pallas kernels, gathered(): pl.pallas_call(gather_kernel, out_shape=(jax.ShapeDtypeStruct((BLOCKS, 4,...  54.9 us
    pallas_call x1, Pallas kernels, body(): pl.pallas_call(update_kernel, out_shape=(jax.ShapeDtypeStruct(factor.shap...  12.7 us
    unnamed x4, local copies, waits for them, and re-layouts  2.03 us

profile of v6, /device:TPU:0, one launch (start us, length us, event | category | flops | bytes accessed | tf_op | source)
XLA Modules:
  0.0 70.2 jit_solution(10430021711767586756)
XLA Ops:
  0.6 0.0 copy-start
  0.6 54.9 %shard_map.68 = (bf16[136,4,4,4,2,128]{5,4,3,2,1,0:T(2,128)(2,1)S(1)}, bf16[2048,512]{1,0:T(8,128)(2,1)S(1)}, bf16[512,2048]{1,0:T(8,128)(2,1)S(1)}, f32[16,8,512]{2,1,0:T(8,128)S(1)}, f32[2,256,256]{2,1,0:T(8,128)S(1)}) custom-call(s32[2]{0:T(128)} %counts_ref.1, bf16[8,4,16,4,2,128]{5,4,3,2,1,0:T(2,128)(2,1)} %bitcast.7, s32[2,16]{1,0:T(2,128)} %margin_ref.3, ...), custom_call_target="tpu_custom_call" | custom-call | flops 2000000000 | bytes 20971520 | tf_op jit(solution)/shard_map/pallas_call | solution.py:413
  55.5 0.0 copy-done
  55.5 12.7 %shard_map.69 = (bf16[2,2048,256]{2,1,0:T(8,128)(2,1)S(1)}, f32[2,2,128,128]{3,2,1,0:T(8,128)S(1)}) custom-call(s32[2,16]{1,0:T(2,128)S(1)} %copy-done, bf16[136,128,128]{2,1,0:T(8,128)(2,1)S(1)} %bitcast.5, bf16[2048,512]{1,0:T(8,128)(2,1)S(1)} %get-tuple-element.8.live_ref, bf16[512,2048]{1,0:T(8,128)(2,1)S(1)} %get-tuple-element.9.flipped_ref, ...), custom_call_target="tpu_custom_call" | custom-call | flops 6000000000 | bytes 20971520 | tf_op jit(solution)/shard_map/pallas_call | solution.py:592
  68.2 1.3 %copy.9 = bf16[2,2048,256]{2,1,0:T(8,128)(2,1)} copy(bf16[2,2048,256]{2,1,0:T(8,128)(2,1)S(1)} %get-tuple-element.14) | data formatting | bytes 4194304
  69.5 0.7 copy.10
Async XLA Ops:
  0.6 54.9 %copy-start = (s32[2,16]{1,0:T(2,128)S(1)}, s32[2,16]{1,0:T(2,128)}, u32[]{:S(2)}) copy-start(s32[2,16]{1,0:T(2,128)} %margin_ref.3) | copy-start | bytes 388

commit v7 on v6

--- a/solution.py
+++ b/solution.py
@@ -11,7 +11,7 @@
 NOV = 16
 BLOCK = 128
 BLOCKS = 136
-CUTS = (0, 3, 16)
+CUTS = (0, 2, 6, 16)
 CHUNKS = len(CUTS) - 1
 SLOTS = 20
 
@@ -451,8 +451,8 @@
 
 
 def update_kernel(
-    margin_ref, sub_ref, live_ref, flipped_ref, alive_ref, local_ref, coupling_ref, diag_ref,
-    ordered, rank_smem, stage, cross_out, cross_in, c_send, c_recv, k_send, k_recv,
+    sub_ref, live_ref, flipped_ref, alive_ref, local_ref, ordered, diag_ref,
+    stage, cross_out, cross_in, c_send, c_recv, k_send, k_recv,
 ):
     front = lax.axis_index("front")
     row = lax.axis_index("row")
@@ -464,13 +464,6 @@
     barrier = pltpu.get_barrier_semaphore()
     for other in (pair_up, pair_down):
         pl.semaphore_signal(barrier, inc=1, device_id=other, device_id_type=MESH)
-
-    def rank(part, _):
-        keys = [order(margin_ref[part, a]) for a in range(NOV)]
-        for a in range(NOV):
-            rank_smem[part, a] = sum((keys[b] < keys[a]).astype(jnp.int32) for b in range(NOV) if b != a)
-        return 0
-
 
     sends = []
 
@@ -522,8 +515,6 @@
         )
 
     own, lent, both = slice(0, 256), slice(256, 512), slice(0, 512)
-    for part in range(2):
-        rank(part, 0)
     order_of_work = [(index, both) for index in range(4)]
     order_of_work += [(index, lent) for index in range(4, 8)]
     order_of_work += [(index, own) for index in range(4, 8)]
@@ -563,14 +554,6 @@
     for number in range(2):
         at = slice(number * BLOCK, (number + 1) * BLOCK)
         diag_ref[mine, number] = local_ref[mine, at, at] - total[at, at]
-    def restore(part):
-        def one(a, _):
-            rows = pl.multiple_of(a * BLOCK, BLOCK)
-            coupling_ref[part, pl.ds(rows, BLOCK), :] = ordered[part, rank_smem[part, a]]
-            return 0
-
-        lax.fori_loop(0, NOV, one, 0, unroll=4)
-
     for number in range(2):
         at = slice(number * BLOCK, (number + 1) * BLOCK)
         pltpu.make_async_copy(cross_in.at[number], cross_in.at[number], k_recv.at[number]).wait()
@@ -579,27 +562,41 @@
         for number in range(2):
             ref = returned(1 - mine, quarter * 4, number)
             pltpu.make_async_copy(ref, ref, c_recv.at[2 * quarter + number]).wait()
-    restore(mine)
-    restore(1 - mine)
     for copy in sends:
         copy.wait_send()
+
+
+def restore_kernel(margin_ref, ordered_ref, diag_in, coupling_ref, diag_ref, sems):
+    diag_copy = pltpu.make_async_copy(diag_in, diag_ref, sems.at[2])
+    diag_copy.start()
+    for part in range(2):
+        keys = [order(margin_ref[part, a]) for a in range(NOV)]
+        for a in range(NOV):
+            at = sum((keys[b] < keys[a]).astype(jnp.int32) for b in range(NOV) if b != a)
+            pltpu.make_async_copy(
+                ordered_ref.at[part, at],
+                coupling_ref.at[part, pl.ds(a * BLOCK, BLOCK)],
+                sems.at[part],
+            ).start()
+    for part in range(2):
+        whole = coupling_ref.at[part]
+        pltpu.make_async_copy(whole, whole, sems.at[part]).wait()
+    diag_copy.wait()
 
 
 def body(parent, margin, counts, factor, local_inverse):
     sub, live, flipped, alive, local = gathered(parent, margin, counts, factor, local_inverse)
     vmem = pl.BlockSpec(memory_space=pltpu.VMEM)
     dma = pltpu.SemaphoreType.DMA
-    return pl.pallas_call(
+    ordered, diag = pl.pallas_call(
         update_kernel,
         out_shape=(
-            jax.ShapeDtypeStruct(factor.shape, jnp.bfloat16),
+            jax.ShapeDtypeStruct((2, NOV, BLOCK, 256), jnp.bfloat16),
             jax.ShapeDtypeStruct((2, 2, BLOCK, BLOCK), jnp.float32),
         ),
-        in_specs=[pl.BlockSpec(memory_space=pltpu.SMEM)] + [vmem] * 5,
+        in_specs=[vmem] * 5,
         out_specs=(vmem, vmem),
         scratch_shapes=[
-            pltpu.VMEM((2, NOV, BLOCK, 256), jnp.bfloat16),
-            pltpu.SMEM((2, NOV), jnp.int32),
             pltpu.VMEM((2, NOV, BLOCK, BLOCK), jnp.bfloat16),
             pltpu.VMEM((2, BLOCK, BLOCK), jnp.float32),
             pltpu.VMEM((2, BLOCK, BLOCK), jnp.float32),
@@ -611,7 +608,19 @@
         cost_estimate=pl.CostEstimate(
             flops=6 * 10**9, bytes_accessed=20 * 2**20, transcendentals=0
         ),
-    )(margin, sub.reshape(BLOCKS, BLOCK, BLOCK), live, flipped, alive, local)
+    )(sub.reshape(BLOCKS, BLOCK, BLOCK), live, flipped, alive, local)
+    hbm = pl.BlockSpec(memory_space=pl.ANY)
+    return pl.pallas_call(
+        restore_kernel,
+        out_shape=(
+            jax.ShapeDtypeStruct(factor.shape, jnp.bfloat16),
+            jax.ShapeDtypeStruct((2, 2, BLOCK, BLOCK), jnp.float32),
+        ),
+        in_specs=[pl.BlockSpec(memory_space=pltpu.SMEM), vmem, vmem],
+        out_specs=(hbm, hbm),
+        scratch_shapes=[dma((3,))],
+        compiler_params=pltpu.CompilerParams(vmem_limit_bytes=8 * 2**20),
+    )(margin, ordered, diag)
 
 
 def solution(mesh):

time: 70.5 us -> 69.5 us (0.986)
  local copies, waits for them, and re-layouts: 2.03 us -> 0.01 us
    unnamed x4 -> x2, local copies, waits for them, and re-layouts: 2.03 us -> 0.01 us
    pallas_call x1 -> x2, Pallas kernels: 12.7 us -> 13.5 us  [the longest x1 11.5 us: body(): pl.pallas_call(update_kernel, out_shape=(jax.ShapeDtypeStruct((2, NOV, BL...]
where the time goes in v7:
time: 69.5 us; the launch traced here: 68.6 us
  Pallas kernels  68 us (98%)
    pallas_call x1, Pallas kernels, gathered(): pl.pallas_call(gather_kernel, out_shape=(jax.ShapeDtypeStruct((BLOCKS, 4,...  54.5 us
    pallas_call x1, Pallas kernels, body(): pl.pallas_call(update_kernel, out_shape=(jax.ShapeDtypeStruct((2, NOV, BL...  11.5 us
    pallas_call x1, Pallas kernels, body(): pl.pallas_call(restore_kernel, out_shape=(jax.ShapeDtypeStruct(factor.sha...  1.97 us

profile of v7, /device:TPU:0, one launch (start us, length us, event | category | flops | bytes accessed | tf_op | source)
XLA Modules:
  0.0 68.6 jit_solution(105783801196845278)
XLA Ops:
  0.6 54.5 %shard_map.68 = (bf16[136,4,4,4,2,128]{5,4,3,2,1,0:T(2,128)(2,1)S(1)}, bf16[2048,512]{1,0:T(8,128)(2,1)S(1)}, bf16[512,2048]{1,0:T(8,128)(2,1)S(1)}, f32[16,8,512]{2,1,0:T(8,128)S(1)}, f32[2,256,256]{2,1,0:T(8,128)S(1)}) custom-call(s32[2]{0:T(128)} %counts_ref.1, bf16[8,4,16,4,2,128]{5,4,3,2,1,0:T(2,128)(2,1)} %bitcast.7, s32[2,16]{1,0:T(2,128)} %margin_ref.3, ...), custom_call_target="tpu_custom_call" | custom-call | flops 2000000000 | bytes 20971520 | tf_op jit(solution)/shard_map/pallas_call | solution.py:413
  55.1 0.0 copy-start
  55.2 11.5 %shard_map.69 = (bf16[2,16,128,256]{3,2,1,0:T(8,128)(2,1)S(1)}, f32[2,2,128,128]{3,2,1,0:T(8,128)S(1)}) custom-call(bf16[136,128,128]{2,1,0:T(8,128)(2,1)S(1)} %bitcast.5, bf16[2048,512]{1,0:T(8,128)(2,1)S(1)} %get-tuple-element.10.live_ref, bf16[512,2048]{1,0:T(8,128)(2,1)S(1)} %get-tuple-element.11.flipped_ref, ...), custom_call_target="tpu_custom_call" | custom-call | flops 6000000000 | bytes 20971520 | tf_op jit(solution)/shard_map/pallas_call | solution.py:591
  66.7 0.0 copy-done
  66.7 2.0 %shard_map.70 = (bf16[2,2048,256]{2,1,0:T(8,128)(2,1)}, f32[2,2,128,128]{3,2,1,0:T(8,128)}) custom-call(s32[2,16]{1,0:T(2,128)S(1)} %copy-done, bf16[2,16,128,256]{3,2,1,0:T(8,128)(2,1)S(1)} %get-tuple-element.14.ordered_ref, f32[2,2,128,128]{3,2,1,0:T(8,128)S(1)} %get-tuple-element.15.diag_in), custom_call_target="tpu_custom_call" | custom-call | tf_op jit(solution)/shard_map/pallas_call | solution.py:613
Async XLA Ops:
  55.1 11.5 %copy-start = (s32[2,16]{1,0:T(2,128)S(1)}, s32[2,16]{1,0:T(2,128)}, u32[]{:S(2)}) copy-start(s32[2,16]{1,0:T(2,128)} %margin_ref.3) | copy-start | bytes 388

commit v8 on v7

--- a/solution.py
+++ b/solution.py
@@ -138,7 +138,7 @@
         )
         return 0
 
-    lax.fori_loop(1, 32, greet, 0)
+    lax.fori_loop(1, 32, greet, 0, unroll=True)
     for other in (sibling, y_up, y_down):
         pl.semaphore_signal(barrier, inc=1, device_id=other, device_id_type=MESH)
     parent_load.wait()
@@ -186,6 +186,20 @@
             pl.when(jnp.logical_and(core == own_core, z == own_z))(
                 functools.partial(spread_all, own_core, own_z)
             )
+
+    factor_load.wait()
+    lends = []
+    for number, device in enumerate((pair_up, pair_down)):
+        copy = pltpu.make_async_remote_copy(
+            src_ref=factor_buf.at[1 - mine, :, :, pl.ds(number * BLOCK, BLOCK)],
+            dst_ref=lent_buf.at[number],
+            send_sem=f_send.at[number],
+            recv_sem=f_recv.at[number],
+            device_id=device,
+            device_id_type=MESH,
+        )
+        copy.start()
+        lends.append(copy)
 
     for source in range(4):
         pltpu.make_async_copy(margin_ref, margin_buf.at[source], m_recv.at[source]).wait()
@@ -246,20 +260,6 @@
 
     for own_core in range(2):
         pl.when(core == own_core)(functools.partial(swap_cores, own_core, False))
-
-    factor_load.wait()
-    lends = []
-    for number, device in enumerate((pair_up, pair_down)):
-        copy = pltpu.make_async_remote_copy(
-            src_ref=factor_buf.at[1 - mine, :, :, pl.ds(number * BLOCK, BLOCK)],
-            dst_ref=lent_buf.at[number],
-            send_sem=f_send.at[number],
-            recv_sem=f_recv.at[number],
-            device_id=device,
-            device_id_type=MESH,
-        )
-        copy.start()
-        lends.append(copy)
 
     for own_core in range(2):
         pl.when(core == 1 - own_core)(functools.partial(swap_cores, own_core, True))
@@ -515,9 +515,9 @@
         )
 
     own, lent, both = slice(0, 256), slice(256, 512), slice(0, 512)
-    order_of_work = [(index, both) for index in range(4)]
-    order_of_work += [(index, lent) for index in range(4, 8)]
-    order_of_work += [(index, own) for index in range(4, 8)]
+    order_of_work = [(index, both) for index in range(5)]
+    order_of_work += [(index, lent) for index in range(5, 8)]
+    order_of_work += [(index, own) for index in range(5, 8)]
     for index, cols in order_of_work:
         halves = pair(index, cols)
         for half in range(2):

time: 69.5 us -> 68.7 us (0.988); the launches traced: 68.6 us -> 68.6 us
  no operation moved by 1% of the time
where the time goes in v8:
time: 68.7 us; the launch traced here: 68.6 us
  Pallas kernels  67.9 us (99%)
    pallas_call x1, Pallas kernels, gathered(): pl.pallas_call(gather_kernel, out_shape=(jax.ShapeDtypeStruct((BLOCKS, 4,...  54.1 us
    pallas_call x1, Pallas kernels, body(): pl.pallas_call(update_kernel, out_shape=(jax.ShapeDtypeStruct((2, NOV, BL...  11.9 us
    pallas_call x1, Pallas kernels, body(): pl.pallas_call(restore_kernel, out_shape=(jax.ShapeDtypeStruct(factor.sha...  1.97 us

profile of v8, /device:TPU:0, one launch (start us, length us, event | category | flops | bytes accessed | tf_op | source)
XLA Modules:
  0.0 68.6 jit_solution(10624051563148050056)
XLA Ops:
  0.6 54.1 %shard_map.68 = (bf16[136,4,4,4,2,128]{5,4,3,2,1,0:T(2,128)(2,1)S(1)}, bf16[2048,512]{1,0:T(8,128)(2,1)S(1)}, bf16[512,2048]{1,0:T(8,128)(2,1)S(1)}, f32[16,8,512]{2,1,0:T(8,128)S(1)}, f32[2,256,256]{2,1,0:T(8,128)S(1)}) custom-call(s32[2]{0:T(128)} %counts_ref.1, bf16[8,4,16,4,2,128]{5,4,3,2,1,0:T(2,128)(2,1)} %bitcast.7, s32[2,16]{1,0:T(2,128)} %margin_ref.3, ...), custom_call_target="tpu_custom_call" | custom-call | flops 2000000000 | bytes 20971520 | tf_op jit(solution)/shard_map/pallas_call | solution.py:413
  54.7 0.0 copy-start
  54.7 11.9 %shard_map.69 = (bf16[2,16,128,256]{3,2,1,0:T(8,128)(2,1)S(1)}, f32[2,2,128,128]{3,2,1,0:T(8,128)S(1)}) custom-call(bf16[136,128,128]{2,1,0:T(8,128)(2,1)S(1)} %bitcast.5, bf16[2048,512]{1,0:T(8,128)(2,1)S(1)} %get-tuple-element.10.live_ref, bf16[512,2048]{1,0:T(8,128)(2,1)S(1)} %get-tuple-element.11.flipped_ref, ...), custom_call_target="tpu_custom_call" | custom-call | flops 6000000000 | bytes 20971520 | tf_op jit(solution)/shard_map/pallas_call | solution.py:591
  66.6 0.0 copy-done
  66.6 2.0 %shard_map.70 = (bf16[2,2048,256]{2,1,0:T(8,128)(2,1)}, f32[2,2,128,128]{3,2,1,0:T(8,128)}) custom-call(s32[2,16]{1,0:T(2,128)S(1)} %copy-done, bf16[2,16,128,256]{3,2,1,0:T(8,128)(2,1)S(1)} %get-tuple-element.14.ordered_ref, f32[2,2,128,128]{3,2,1,0:T(8,128)S(1)} %get-tuple-element.15.diag_in), custom_call_target="tpu_custom_call" | custom-call | tf_op jit(solution)/shard_map/pallas_call | solution.py:613
Async XLA Ops:
  54.7 11.9 %copy-start = (s32[2,16]{1,0:T(2,128)S(1)}, s32[2,16]{1,0:T(2,128)}, u32[]{:S(2)}) copy-start(s32[2,16]{1,0:T(2,128)} %margin_ref.3) | copy-start | bytes 388

commit v9 on v8

--- a/solution.py
+++ b/solution.py
@@ -179,7 +179,7 @@
                 ).start()
                 return 0
 
-            lax.fori_loop(0 if offset else 1, 8, spread, 0)
+            lax.fori_loop(0 if offset else 1, 8, spread, 0, unroll=True)
 
     for own_core in range(2):
         for own_z in range(4):

time: 68.7 us -> 68.9 us (level)
  no operation moved by 1% of the time
where the time goes in v9:
time: 68.9 us; the launch traced here: 68.8 us
  Pallas kernels  67.9 us (99%)
  between operations  0.82 us (1%)
    pallas_call x1, Pallas kernels, gathered(): pl.pallas_call(gather_kernel, out_shape=(jax.ShapeDtypeStruct((BLOCKS, 4,...  54 us
    pallas_call x1, Pallas kernels, body(): pl.pallas_call(update_kernel, out_shape=(jax.ShapeDtypeStruct((2, NOV, BL...  11.9 us
    pallas_call x1, Pallas kernels, body(): pl.pallas_call(restore_kernel, out_shape=(jax.ShapeDtypeStruct(factor.sha...  1.97 us

profile of v9, /device:TPU:0, one launch (start us, length us, event | category | flops | bytes accessed | tf_op | source)
XLA Modules:
  0.0 68.8 jit_solution(5671615014176515774)
XLA Ops:
  0.6 54.0 %shard_map.68 = (bf16[136,4,4,4,2,128]{5,4,3,2,1,0:T(2,128)(2,1)S(1)}, bf16[2048,512]{1,0:T(8,128)(2,1)S(1)}, bf16[512,2048]{1,0:T(8,128)(2,1)S(1)}, f32[16,8,512]{2,1,0:T(8,128)S(1)}, f32[2,256,256]{2,1,0:T(8,128)S(1)}) custom-call(s32[2]{0:T(128)} %counts_ref.1, bf16[8,4,16,4,2,128]{5,4,3,2,1,0:T(2,128)(2,1)} %bitcast.7, s32[2,16]{1,0:T(2,128)} %margin_ref.3, ...), custom_call_target="tpu_custom_call" | custom-call | flops 2000000000 | bytes 20971520 | tf_op jit(solution)/shard_map/pallas_call | solution.py:413
  54.7 0.0 copy-start
  54.7 11.9 %shard_map.69 = (bf16[2,16,128,256]{3,2,1,0:T(8,128)(2,1)S(1)}, f32[2,2,128,128]{3,2,1,0:T(8,128)S(1)}) custom-call(bf16[136,128,128]{2,1,0:T(8,128)(2,1)S(1)} %bitcast.5, bf16[2048,512]{1,0:T(8,128)(2,1)S(1)} %get-tuple-element.10.live_ref, bf16[512,2048]{1,0:T(8,128)(2,1)S(1)} %get-tuple-element.11.flipped_ref, ...), custom_call_target="tpu_custom_call" | custom-call | flops 6000000000 | bytes 20971520 | tf_op jit(solution)/shard_map/pallas_call | solution.py:591
  66.6 0.0 copy-done
  66.6 2.0 %shard_map.70 = (bf16[2,2048,256]{2,1,0:T(8,128)(2,1)}, f32[2,2,128,128]{3,2,1,0:T(8,128)}) custom-call(s32[2,16]{1,0:T(2,128)S(1)} %copy-done, bf16[2,16,128,256]{3,2,1,0:T(8,128)(2,1)S(1)} %get-tuple-element.14.ordered_ref, f32[2,2,128,128]{3,2,1,0:T(8,128)S(1)} %get-tuple-element.15.diag_in), custom_call_target="tpu_custom_call" | custom-call | tf_op jit(solution)/shard_map/pallas_call | solution.py:613
Async XLA Ops:
  54.7 11.9 %copy-start = (s32[2,16]{1,0:T(2,128)S(1)}, s32[2,16]{1,0:T(2,128)}, u32[]{:S(2)}) copy-start(s32[2,16]{1,0:T(2,128)} %margin_ref.3) | copy-start | bytes 388
